TPU v7x, 128 devices: a whole 4x4x4 slice. The times are simulated.
128 devices in a mesh: fsdp: 8 (over y, z_hi), expert: 16 (over z_lo, x, core).
Axes of the slice: x: 4, y: 4, z: 4 (z_hi: 2, z_lo: 2; z = z_hi * 2 + z_lo), core: 2. Of those that a mesh axis runs over, the one named last changes fastest.
Arguments:
- tokens: bfloat16 [1024, 5120], P(('fsdp', 'expert')), may hold values from -6 to 6
- gate_scores: bfloat16 [1024, 6], P(('fsdp', 'expert')), may hold values from 0.049804688 to 0.59765625
- expert_ids: int32 [1024, 6], P(('fsdp', 'expert')), may hold values from 0 to 63, all different within a row; in each aligned block of 8 rows (0 to 7, 8 to 15, ...) at most 2 rows name the same one
- expert_gate: bfloat16 [128, 5120, 768], P(('fsdp', 'expert')), may hold values from -0.078125 to 0.078125
- expert_up: bfloat16 [128, 5120, 768], P(('fsdp', 'expert')), may hold values from -0.078125 to 0.078125
- expert_down: bfloat16 [128, 768, 5120], P(('fsdp', 'expert')), may hold values from -0.15625 to 0.15625
- shared_gate: bfloat16 [5120, 3072], P('expert', 'fsdp'), may hold values from -0.078125 to 0.078125
- shared_up: bfloat16 [5120, 3072], P('expert', 'fsdp'), may hold values from -0.078125 to 0.078125
- shared_down: bfloat16 [3072, 5120], P('fsdp', 'expert'), may hold values from -0.109375 to 0.109375
Outputs:
- mixed: bfloat16 [1024, 5120], P(('fsdp', 'expert'))
Inputs may be any that keep to these rules, and one draw needn't show every extreme that they name: `expert_ids`: each row names 6 different experts. Within the 8 rows of one device no expert is named by more than 2 rows, a bound that some block reaches.
All inputs are finite; a program needn't handle non-finite values.
Results may differ from a plain program's by a relative error of at most 0.0053.
Values may be sent and summed in bfloat16 or wider, within the bound.
A program may use at most 128 MiB of HBM per device.

v0:
```python
import jax
import jax.numpy as jnp
from jax import lax
from jax.sharding import PartitionSpec as P


def silu_product(row_data, w_gate, w_up):
    gate_act = jnp.dot(row_data, w_gate, preferred_element_type=jnp.float32)
    up_proj = jnp.dot(row_data, w_up, preferred_element_type=jnp.float32)
    return (jax.nn.silu(gate_act) * up_proj).astype(jnp.bfloat16)


def slot_of(flat_ids, expert_count):
    onehot = (flat_ids[:, None] == jnp.arange(expert_count, dtype=jnp.int32)[None, :]).astype(
        jnp.int32
    )
    before = jnp.cumsum(onehot, axis=0) - onehot
    return jnp.sum(before * onehot, axis=1)


def fill_rows(row_data, dest_index, slot_total, pick_count):
    pair_token = jnp.arange(dest_index.shape[0], dtype=jnp.int32) // pick_count
    source = jnp.full((slot_total,), -1, jnp.int32).at[dest_index].set(pair_token)
    is_valid = source >= 0
    picked = jnp.take(row_data, jnp.maximum(source, 0), axis=0)
    return jnp.where(is_valid[:, None], picked, jnp.zeros_like(picked))


def expert_rows(row_block, w_gate, w_up, w_down):
    block_shape = row_block.shape
    flat_rows = row_block.reshape(-1, block_shape[-1])
    hidden = silu_product(flat_rows, w_gate, w_up)
    result = jnp.dot(hidden, w_down, preferred_element_type=jnp.float32).astype(jnp.bfloat16)
    return result.reshape(block_shape)


def local(
    tokens,
    gate_scores,
    expert_ids,
    expert_gate,
    expert_up,
    expert_down,
    shared_gate,
    shared_up,
    shared_down,
):
    expert_width = lax.axis_size("expert")
    fsdp_width = lax.axis_size("fsdp")
    device_count = expert_width * fsdp_width
    expert_count = device_count // 2
    tok_dev, pick_count = expert_ids.shape
    model_width = tokens.shape[1]
    capacity = min(tok_dev, max(2, 2 * tok_dev * pick_count // expert_count))
    w_gate = expert_gate[0]
    w_up = expert_up[0]
    w_down = expert_down[0]
    flat_ids = expert_ids.reshape(-1)
    slot_place = flat_ids * capacity + slot_of(flat_ids, expert_count)
    own_block = fill_rows(tokens, slot_place, expert_count * capacity, pick_count)
    own_block = own_block.reshape(expert_count, 1, capacity, model_width)
    outgoing = jnp.broadcast_to(own_block, (expert_count, 2, capacity, model_width))
    outgoing = outgoing.reshape(device_count, capacity, model_width)
    partial_value = expert_rows(
        lax.all_to_all(outgoing, ("fsdp", "expert"), split_axis=0, concat_axis=0, tiled=True),
        w_gate,
        w_up,
        w_down,
    )
    returned = lax.all_to_all(
        partial_value, ("fsdp", "expert"), split_axis=0, concat_axis=0, tiled=True
    )
    halves = returned.reshape(expert_count, 2, capacity, model_width)
    half_sums = (halves[:, 0].astype(jnp.float32) + halves[:, 1].astype(jnp.float32)).reshape(
        -1, model_width
    )
    picked = jnp.take(half_sums, slot_place, axis=0).reshape(tok_dev, pick_count, model_width)
    weights = gate_scores.astype(jnp.float32)
    routed = jnp.zeros((tok_dev, model_width), jnp.float32)
    for pick_idx in range(pick_count):
        routed = routed + picked[:, pick_idx] * weights[:, pick_idx : pick_idx + 1]
    col_tokens = lax.all_gather(tokens, "fsdp", axis=0, tiled=True)
    gate_act = jnp.dot(
        col_tokens,
        lax.all_gather(shared_gate, "expert", axis=0, tiled=True),
        preferred_element_type=jnp.float32,
    )
    up_proj = jnp.dot(
        col_tokens,
        lax.all_gather(shared_up, "expert", axis=0, tiled=True),
        preferred_element_type=jnp.float32,
    )
    shared_hidden = (jax.nn.silu(gate_act) * up_proj).astype(jnp.bfloat16)
    shared_part = jnp.dot(
        shared_hidden,
        lax.all_gather(shared_down, "expert", axis=1, tiled=True),
        preferred_element_type=jnp.float32,
    )
    shared_out = lax.psum_scatter(shared_part, "fsdp", scatter_dimension=0, tiled=True)
    return (routed + shared_out).astype(jnp.bfloat16)


def solution(mesh):
    return jax.shard_map(
        local,
        mesh=mesh,
        in_specs=(
            P(("fsdp", "expert"), None),
            P(("fsdp", "expert"), None),
            P(("fsdp", "expert"), None),
            P(("fsdp", "expert"), None, None),
            P(("fsdp", "expert"), None, None),
            P(("fsdp", "expert"), None, None),
            P("expert", "fsdp"),
            P("expert", "fsdp"),
            P("fsdp", "expert"),
        ),
        out_specs=P(("fsdp", "expert"), None),
        check_vma=False,
    )
```

profile of v0, /device:TPU:1, one launch (start us, length us, event | category | flops | bytes accessed | tf_op | source)
XLA Modules:
  0.0 271.7 jit_solution(4362859196413473284)
XLA Ops:
  6.5 0.7 all-gather.4.cloned.1.call-update
  7.3 0.7 all-gather.6.cloned.1.call-update
  8.1 0.7 all-gather.8.cloned.1.call-update
  8.7 0.8 reshape.91
  9.5 0.7 broadcast_multiply_fusion
  10.4 0.2 select_reduce_fusion
  10.6 0.7 scatter_custom_fusion
  11.4 0.1 broadcast_in_dim.50
  11.6 0.2 broadcast_in_dim.52
  11.7 1.3 gather_fusion
  13.0 0.5 gather.13
  13.6 1.9 broadcast_select_fusion.1
  15.5 1.4 broadcast_in_dim.57
  16.8 56.5 %all_to_all.10 = bf16[128,2,5120]{2,1,0:T(2,128)(2,1)S(1)} all-to-all(bf16[128,2,5120]{2,1,0:T(2,128)(2,1)S(1)} %bitcast.91), channel_id=1, replica_groups=mesh['fsdp'=8,'expert'=16] {'fsdp','expert'}, dimensions={0} | all-to-all | bytes 5242880 | tf_op jit(solution)/shard_map/all_to_all | solution.py:65
  73.4 2.5 reshape.93
  75.9 7.2 %fusion.4 = f32[256,768]{1,0:T(8,128)} fusion(bf16[256,5120]{1,0:T(8,128)(2,1)} %reshape.93, bf16[1,5120,768]{2,1,0:T(8,128)(2,1)} %param.12), kind=kOutput, calls=%fused_computation.7 | convolution fusion | flops 2013265920 | bytes 11272192 | tf_op jit(solution)/shard_map/dot_general | solution.py:8
  83.1 12.7 %fusion.6 = bf16[256,5120]{1,0:T(8,128)(2,1)} fusion(bf16[1,768,5120]{2,1,0:T(8,128)(2,1)} %param.14, bf16[256,5120]{1,0:T(8,128)(2,1)S(1)} %copy-done.1, bf16[1,5120,768]{2,1,0:T(8,128)(2,1)} %param.13, f32[256,768]{1,0:T(8,128)} %fusion.4), kind=kOutput, calls=%fused_computation.9 | convolution fusion | flops 4029022208 | bytes 21757952 | tf_op jit(solution)/shard_map/dot_general | solution.py:33
  95.8 6.3 %reshape.94 = bf16[128,2,5120]{2,1,0:T(2,128)(2,1)} reshape(bf16[256,5120]{1,0:T(8,128)(2,1)} %fusion.6) | data formatting | bytes 5242880 | tf_op jit(solution)/shard_map/reshape | solution.py:34
  102.1 4.8 %all-to-all-start.1 = ((bf16[128,2,5120]{2,1,0:T(2,128)(2,1)}), bf16[128,2,5120]{2,1,0:T(2,128)(2,1)S(1)}, u32[]{:S(2)}, u32[]{:S(2)}) async-start(bf16[128,2,5120]{2,1,0:T(2,128)(2,1)} %reshape.94), calls=%async_computation.1 | async-start | bytes 5242880 | tf_op jit(solution)/shard_map/all_to_all | solution.py:70
  107.1 57.9 %all_gather.12 = bf16[64,5120]{1,0:T(8,128)(2,1)S(1)} all-gather(bf16[8,5120]{1,0:T(8,128)(2,1)S(1)} %copy-done), channel_id=1, replica_groups=mesh['fsdp'=8,'expert'=16] {'fsdp'}, dimensions={0}, use_global_device_ids=true | all-gather | bytes 737280 | tf_op jit(solution)/shard_map/all_gather | solution.py:82
  165.0 2.9 %fusion.45 = f32[64,384]{1,0:T(8,128)S(1)} fusion(bf16[64,5120]{1,0:T(8,128)(2,1)S(1)} %all_gather.12, bf16[5120,384]{1,0:T(8,128)(2,1)} %all-gather.4.cloned.1.call-done), kind=kOutput, calls=%fused_computation.75 | convolution fusion | flops 251658240 | bytes 4685824 | tf_op jit(solution)/shard_map/dot_general | solution.py:83
  168.0 16.5 %all-gather.8.cloned.1.call-done = bf16[384,5120]{0,1:T(8,128)(2,1)} async-done(((bf16[384,320]{0,1:T(8,128)(2,1)}), bf16[384,5120]{0,1:T(8,128)(2,1)}) %all-gather.8.cloned.1.call-update) | async-done | bytes 3932176 | tf_op jit(solution)/shard_map/all_gather | solution.py:96
  184.5 6.7 %fusion.16 = f32[64,5120]{1,0:T(8,128)} fusion(bf16[384,5120]{0,1:T(8,128)(2,1)} %all-gather.8.cloned.1.call-done, bf16[64,5120]{1,0:T(8,128)(2,1)S(1)} %all_gather.12, bf16[5120,384]{1,0:T(8,128)(2,1)} %all-gather.6.cloned.1.call-done, f32[64,384]{1,0:T(8,128)S(1)} %fusion.45), kind=kOutput, calls=%fused_computation.19 | convolution fusion | flops 503463936 | bytes 9928704 | tf_op jit(solution)/shard_map/dot_general | solution.py:94
  191.3 0.1 copy.13
  191.4 0.3 slice_reduce_fusion.5
  191.7 2.9 %convert_add_fusion = f32[64,1,2,5120]{3,2,0,1:T(2,128)} fusion(bf16[64,2,2,5120]{3,2,1,0:T(2,128)(2,1)S(1)} %bitcast.90), kind=kLoop, calls=%fused_computation.10 | loop fusion | flops 1966080 | bytes 5242880 | tf_op jit(solution)/shard_map/add | solution.py:74
  194.5 3.3 %add.87 = f32[128,5120]{1,0:T(8,128)S(1)} reshape(f32[64,1,2,5120]{3,2,0,1:T(2,128)} %convert_add_fusion) | data formatting | bytes 5242880 | tf_op jit(solution)/shard_map/add | solution.py:74
  197.8 1.8 gather_fusion.1
  199.6 1.4 gather.15
  201.0 0.6 copy_select_fusion
  201.7 61.8 %reduce-scatter.2.cloned.1.call-done = f32[8,5120]{1,0:T(8,128)} async-done(((f32[64,5120]{1,0:T(8,128)}), f32[8,5120]{1,0:T(8,128)}) %reduce-scatter.2.cloned.1.call-update) | async-done | bytes 163856 | tf_op jit(solution)/shard_map/reduce_scatter | solution.py:99
  263.5 1.7 fusion.23
  (28 shorter events, 0.5 us)
Async XLA Ops:
  6.5 5.2 %copy-start = (bf16[8,5120]{1,0:T(8,128)(2,1)S(1)}, bf16[8,5120]{1,0:T(8,128)(2,1)}, u32[]{:S(2)}) copy-start(bf16[8,5120]{1,0:T(8,128)(2,1)} %param.9) | copy-start | bytes 245764
  6.5 158.5 %all-gather.4.cloned.1.call-start = ((), (), s32[]{:S(2)}) async-start(), calls=%async_computation.3 | async-start | bytes 4177920 | tf_op jit(solution)/shard_map/all_gather | solution.py:85
  7.3 160.7 %all-gather.6.cloned.1.call-start = ((), (), s32[]{:S(2)}) async-start(), calls=%async_computation.4 | async-start | bytes 4177920 | tf_op jit(solution)/shard_map/all_gather | solution.py:90
  8.0 176.5 %all-gather.8.cloned.1.call-start = ((), (), s32[]{:S(2)}) async-start(), calls=%async_computation.5 | async-start | bytes 4177920 | tf_op jit(solution)/shard_map/all_gather | solution.py:96
  75.9 7.3 %copy-start.1 = (bf16[256,5120]{1,0:T(8,128)(2,1)S(1)}, bf16[256,5120]{1,0:T(8,128)(2,1)}, u32[]{:S(2)}) copy-start(bf16[256,5120]{1,0:T(8,128)(2,1)} %reshape.93) | copy-start | bytes 7864324
  102.1 89.5 %all-to-all-start.1 = ((bf16[128,2,5120]{2,1,0:T(2,128)(2,1)}), bf16[128,2,5120]{2,1,0:T(2,128)(2,1)S(1)}, u32[]{:S(2)}, u32[]{:S(2)}) async-start(bf16[128,2,5120]{2,1,0:T(2,128)(2,1)} %reshape.94), calls=%async_computation.1 | async-start | bytes 5242880 | tf_op jit(solution)/shard_map/all_to_all | solution.py:70
  107.0 156.5 %reduce-scatter.2.cloned.1.call-start = ((), (), s32[]{:S(2)}) async-start(), calls=%async_computation.6 | async-start | bytes 1474560 | tf_op jit(solution)/shard_map/reduce_scatter | solution.py:99
  167.9 23.4 %copy-start.2 = (s32[8,6]{1,0:T(8,128)S(1)}, s32[8,6]{1,0:T(8,128)}, u32[]{:S(2)}) copy-start(s32[8,6]{1,0:T(8,128)} %param.11) | copy-start | bytes 580
  167.9 23.5 %copy-start.3 = (bf16[8,6]{1,0:T(8,128)(2,1)S(1)}, bf16[8,6]{1,0:T(8,128)(2,1)}, u32[]{:S(2)}) copy-start(bf16[8,6]{1,0:T(8,128)(2,1)} %param.10) | copy-start | bytes 292
Sparse Core Ops, SparseCore 0:
  9.1 65.4 all-gather.3
  76.3 67.0 all-gather.5
  145.1 39.3 all-gather.7
  191.4 72.0 reduce-scatter.1
where the time goes:
time: 273 us; the launch traced here: 272 us
  blocking collectives  114 us (42%)
  waiting for transfers between devices  80.5 us (29%)
  matrix products  29.6 us (11%)
  local copies, waits for them, and re-layouts  20.8 us (8%)
  between operations  13.3 us (5%)
  other arithmetic  8.13 us (3%)
  starting transfers between devices  4.96 us (2%)
    reduce_scatter x1, waiting for transfers between devices, local(): lax.psum_scatter(shared_part, 'fsdp', scatter_dimension=0, tiled=True)  61.8 us
    all_gather x1, blocking collectives, local(): col_tokens = lax.all_gather(tokens, 'fsdp', axis=0, tiled=True)  57.9 us
    all_to_all x1, blocking collectives, local(): lax.all_to_all(outgoing, ('fsdp', 'expert'), split_axis=0, concat_axis=0,...  56.5 us
    all_gather x1, waiting for transfers between devices, local(): lax.all_gather(shared_down, 'expert', axis=1, tiled=True)  16.5 us
    dot_general x1, matrix products, expert_rows(): jnp.dot(hidden, w_down, preferred_element_type=jnp.float32)  12.7 us
    dot_general x1, matrix products, silu_product(): gate_act = jnp.dot(row_data, w_gate, preferred_element_type=jnp.float32)  7.25 us
    dot_general x1, matrix products, local(): jnp.dot(shared_hidden, lax.all_gather(shared_down, 'expert', axis=1, tile...  6.74 us
    reshape x1, local copies, waits for them, and re-layouts, expert_rows(): return result.reshape(block_shape)  6.29 us
  transfers between devices with their start and end apart: 5, of which 2 were waited for; matrix products, arithmetic and copies ran while one was open for 21% of the time, Pallas kernels for 0%

commit v1 on v0

v1 whole, which is shorter than its diff:
```python
import functools

import jax
import jax.numpy as jnp
from jax import lax
from jax.experimental import pallas as pl
from jax.experimental.pallas import tpu as pltpu
from jax.sharding import PartitionSpec as P

MESH = pl.DeviceIdType.MESH
BF, F32 = jnp.bfloat16, jnp.float32
D, EXT, WID = 5120, 256, 896
DX = D + EXT
HALF, SHF, WIN = 768, 384, 384
ORDERS = ((0, 1, 2), (1, 2, 0), (2, 0, 1))
TN, NT, NN = (((0,), (0,)), ((), ())), (((1,), (1,)), ((), ())), (((1,), (0,)), ((), ()))


def mm(a, b, dims=NN):
    return lax.dot_general(a, b, dims, preferred_element_type=F32)


def kernel(
    tok, ext, wg_h, wu_h, wd_h, sg, su, sd, out,
    T, stage, sib, wg, wu, wd, WS, WR, WA, HT, PM, CM, ag, au, H, RO, PS, PR,
    DB, RA, SA, RB, SB, RC, SD, SDR, SZ, SZR, SQ, SHR, SHA, FO,
    lsem, s_sib, s_ag, r_ag, s_fw, r_fw, s_w, r_w, s_h, r_h, s_sd, r_sd, s_q, r_q, s_p, r_p,
    s_rs, r_rs, s_f, r_f, s_rel, r_rel,
):
    f, e = lax.axis_index("fsdp"), lax.axis_index("expert")
    c = lax.rem(e, 2)
    y, x = f // 2, lax.rem(e // 2, 4)
    zh, zl = lax.rem(f, 2), e // 8
    pos = (y, zh * 2 + zl, x)
    chip = (y * 4 + pos[1]) * 4 + x
    mine = zl * 4 + x

    def dev(p, core):
        return (p[0] * 2 + p[1] // 2, (lax.rem(p[1], 2) * 4 + p[2]) * 2 + core)

    def peer(axis, dist):
        p = list(pos)
        p[axis] = lax.rem(p[axis] + dist, 4)
        return dev(p, c)

    def group(i):
        zz, xx = lax.rem(zl + i // 4, 2), lax.rem(x + i % 4, 4)
        return dev((y, zh * 2 + zz, xx), c), zz * 4 + xx

    def cols(g, core):
        return pl.ds(pl.multiple_of(g * 2 * WID + core * WID, 128), WID)

    sibling = dev(pos, 1 - c)

    def remote(src, dst, ss, rs, to):
        return pltpu.make_async_remote_copy(
            src_ref=src, dst_ref=dst, send_sem=ss, recv_sem=rs, device_id=to, device_id_type=MESH
        )

    pend = []

    def go(cp):
        cp.start()
        pend.append(cp)
        return cp

    loads = [
        pltpu.make_async_copy(wg_h.at[0], wg, lsem.at[0]),
        pltpu.make_async_copy(wu_h.at[0], wu, lsem.at[1]),
        pltpu.make_async_copy(wd_h.at[0], wd.at[:, pl.ds(0, D)], lsem.at[2]),
    ]
    barrier = pltpu.get_barrier_semaphore()
    partners = [peer(a, d) for a in range(3) for d in (1, 2, 3)]
    partners += [group(i)[0] for i in (5, 6, 7)] + [sibling]
    for to in partners:
        pl.semaphore_signal(barrier, inc=1, device_id=to, device_id_type=MESH)

    rows16 = lax.broadcasted_iota(jnp.int32, (16, 1), 0) // 8 == c
    v = tok[...].astype(F32)
    stage[:, pl.ds(0, D)] = jnp.where(rows16, jnp.concatenate([v, v], 0), 0.0).astype(BF)
    v = ext[...].astype(F32)
    stage[:, pl.ds(D, EXT)] = jnp.where(rows16, jnp.concatenate([v, v], 0), 0.0).astype(BF)
    wd[:, pl.ds(D, EXT)] = jnp.zeros((HALF, EXT), BF)
    pl.semaphore_wait(barrier, len(partners))
    cp = go(remote(stage, sib, s_sib.at[0], s_sib.at[1], sibling))
    for ld in loads:
        ld.start()
    cp.wait_recv()
    T[pos[0], pos[1], pos[2]] = stage[...] + sib[...]

    def view(ref, order, depth, col):
        ix = [slice(None)] * 3
        for a in order[depth:]:
            ix[a] = pos[a]
        return ref.at[ix[0], ix[1], ix[2], :, col]

    def from_view(ref, order, depth, dist, col):
        ix = [slice(None)] * 3
        for a in order[depth:]:
            ix[a] = pos[a]
        ix[order[depth]] = lax.rem(pos[order[depth]] + 4 - dist, 4)
        return ref.at[ix[0], ix[1], ix[2], :, col]

    sent = {}

    def ag_send(g, s):
        for d in (1, 2, 3):
            src = view(T, ORDERS[g], s, cols(g, c))
            sent[g, s, d] = go(
                remote(src, src, s_ag.at[g, s, d - 1], r_ag.at[g, s, d - 1], peer(ORDERS[g][s], d))
            )

    fwd = []

    def ag_recv(g, s):
        for d in (1, 2, 3):
            sent[g, s, d].wait_recv()
            part = from_view(T, ORDERS[g], s, d, cols(g, c))
            fwd.append(go(remote(part, part, s_fw.at[g, s, d - 1], r_fw.at[g, s, d - 1], sibling)))

    for g in range(3):
        ag_send(g, 0)

    k_at = lax.broadcasted_iota(jnp.int32, (320, WIN), 0)
    l_at = lax.broadcasted_iota(jnp.int32, (320, WIN), 1)
    shift = (l_at == k_at + 64 * c).astype(F32).astype(BF)
    wt = mm(sg[...], shift, TN).astype(BF)
    for j in range(8):
        WS[j, pl.ds(0, 48)] = wt[48 * j : 48 * j + 48]
    wt = mm(su[...], shift, TN).astype(BF)
    for j in range(8):
        WS[j, pl.ds(48, 48)] = wt[48 * j : 48 * j + 48]
    w_sent = []
    for i in range(1, 8):
        to, j = group(i)
        w_sent.append(go(remote(WS.at[j], WR.at[mine, c], s_w.at[i - 1], r_w.at[i - 1], to)))
    WR[mine, c] = WS[mine]
    sdp = mm(sd[...], shift).astype(BF)

    for s in (1, 2):
        for g in range(3):
            ag_recv(g, s - 1)
            ag_send(g, s)
    for cp in w_sent:
        cp.wait_recv()
    rel = go(remote(WR.at[:, c], WR.at[:, c], s_rel.at[0], r_rel.at[0], sibling))
    rel.wait_recv()
    for j in range(8):
        o = 640 * j
        WA[:, pl.ds(o, 256)] = WR[j, 0, :, pl.ds(0, 256)]
        WA[:, pl.ds(o + 256, 128)] = WR[j, 0, :, pl.ds(256, 128)] + WR[j, 1, :, pl.ds(0, 128)]
        WA[:, pl.ds(o + 384, 256)] = WR[j, 1, :, pl.ds(128, 256)]
    for g in range(3):
        ag_recv(g, 2)
    for cp in fwd:
        cp.wait_recv()

    def gate_up(i, acc):
        col = pl.ds(pl.multiple_of(i * 640, 128), 640)
        t = T[pl.ds(2 * c, 2), :, :, :, col].reshape(512, 640)
        return acc + mm(WA[:, col], t, NT)

    acc = lax.fori_loop(0, 8, gate_up, jnp.zeros((96, 512), F32))
    HT[c, mine] = (jax.nn.silu(acc[:48]) * acc[48:]).astype(BF)
    h_sent = []
    for i in range(1, 8):
        to, j = group(i)
        h_sent.append(go(remote(HT.at[c, mine], HT.at[c, mine], s_h.at[i - 1], r_h.at[i - 1], to)))

    info = T[:, :, :, :, pl.ds(D, 128)].reshape(1024, 128).astype(F32).T
    hit = (info[0:8] == chip.astype(F32)).astype(F32)
    weight = jnp.sum(hit * info[8:16], axis=0, keepdims=True)
    hit = jnp.sum(hit, axis=0, keepdims=True)
    lane = lax.broadcasted_iota(jnp.int32, (8, 1024), 1)
    run = jnp.broadcast_to(hit, (8, 1024))
    for b in range(10):
        run = run + jnp.where(lane >= (1 << b), pltpu.roll(run, 1 << b, 1), 0.0)
    place = run[0:1] - 1.0
    slot = lax.broadcasted_iota(jnp.int32, (256, 1024), 0).astype(F32)
    pm = jnp.where(slot == place, hit, 0.0)
    PM[...] = pm.astype(BF)
    CM[...] = (pm * weight).T.astype(BF)

    ag[...] = jnp.zeros_like(ag)
    au[...] = jnp.zeros_like(au)
    loads[0].wait()
    loads[1].wait()

    def routed_in(i, _):
        col = pl.ds(pl.multiple_of(i * 640, 128), 640)
        xs = mm(PM[...], T[:, :, :, :, col].reshape(1024, 640)).astype(BF)
        ag[...] += mm(xs, wg[col, :])
        au[...] += mm(xs, wu[col, :])
        return 0

    lax.fori_loop(0, 8, routed_in, 0)
    H[...] = (jax.nn.silu(ag[...]) * au[...]).astype(BF)

    for cp in h_sent:
        cp.wait_recv()
    rel = go(remote(HT.at[c], HT.at[c], s_rel.at[1], r_rel.at[1], sibling))

    loads[2].wait()
    p_sent = []
    for g in range(3):
        PS[g] = mm(H[...], wd[:, cols(g, 1 - c)]).astype(BF)
        p_sent.append(go(remote(PS.at[g], PR.at[g], s_p.at[g], r_p.at[g], sibling)))

    rel.wait_recv()
    for t in range(2):
        part = mm(HT[t].reshape(SHF, 512), sdp, TN).astype(BF)
        for k in range(2):
            SD[2 * t + k] = part[256 * k : 256 * k + 256]
    sd_sent = []
    for d in (1, 2, 3):
        at = lax.rem(y + d, 4)
        sd_sent.append(go(remote(SD.at[at], SDR.at[d - 1], s_sd.at[d - 1], r_sd.at[d - 1], peer(0, d))))

    for g in range(3):
        RO[g] = mm(H[...], wd[:, cols(g, c)]).astype(BF)
    rs = {}
    for g in range(3):
        p_sent[g].wait_recv()
        both = (RO[g].astype(F32) + PR[g].astype(F32)).astype(BF)
        for k in range(4):
            DB[g, k] = mm(CM[pl.ds(256 * k, 256)], both).astype(BF).reshape(4, 4, 16, WID)
        a = ORDERS[g][2]
        for d in (1, 2, 3):
            ix = [slice(None)] * 3
            ix[a] = lax.rem(pos[a] + d, 4)
            rs[g, 0, d] = go(
                remote(DB.at[g, ix[0], ix[1], ix[2]], RA.at[g, d - 1], s_rs.at[g, 0, d - 1], r_rs.at[g, 0, d - 1], peer(a, d))
            )

    for cp in sd_sent:
        cp.wait_recv()
    tot = SD[y].astype(F32)
    for d in range(3):
        tot = tot + SDR[d].astype(F32)
    tot = tot.astype(BF)
    SZ[0] = tot[:128]
    SZ[1] = tot[128:]
    z_sent = go(remote(SZ.at[1 - zh], SZR, s_sd.at[3], r_sd.at[3], peer(1, 2)))
    z_sent.wait_recv()
    SQ[...] = (SZ[zh].astype(F32) + SZR[...].astype(F32)).astype(BF).reshape(8, 16, WIN)
    q_sent = []
    for i in range(1, 8):
        to, j = group(i)
        q_sent.append(go(remote(SQ.at[j], SHR.at[mine, c], s_q.at[i - 1], r_q.at[i - 1], to)))
    SHR[mine, c] = SQ[mine]

    for g in range(3):
        for d in (1, 2, 3):
            rs[g, 0, d].wait_recv()
        a3, a2 = ORDERS[g][2], ORDERS[g][1]
        rest = [a for a in range(3) if a != a3]
        for k in range(4):
            ix = [slice(None)] * 3
            ix[a3] = pos[a3]
            ix[rest[0]] = k
            tot = DB[(g, *ix)].astype(F32)
            for d in range(3):
                tot = tot + RA[g, d, k].astype(F32)
            SA[g, k] = tot.astype(BF)
        first = rest[0] == a2
        for d in (1, 2, 3):
            at = lax.rem(pos[a2] + d, 4)
            src = SA.at[g, at] if first else SA.at[g, :, at]
            rs[g, 1, d] = go(remote(src, RB.at[g, d - 1], s_rs.at[g, 1, d - 1], r_rs.at[g, 1, d - 1], peer(a2, d)))
    for cp in q_sent:
        cp.wait_recv()
    rel2 = go(remote(SHR.at[:, c], SHR.at[:, c], s_rel.at[2], r_rel.at[2], sibling))
    for g in range(3):
        for d in (1, 2, 3):
            rs[g, 1, d].wait_recv()
        a3, a2, a1 = ORDERS[g][2], ORDERS[g][1], ORDERS[g][0]
        rest = [a for a in range(3) if a != a3]
        tot = (SA[g, pos[a2]] if rest[0] == a2 else SA[g, :, pos[a2]]).astype(F32)
        for d in range(3):
            tot = tot + RB[g, d].astype(F32)
        SB[g] = tot.astype(BF)
        for d in (1, 2, 3):
            at = lax.rem(pos[a1] + d, 4)
            rs[g, 2, d] = go(
                remote(SB.at[g, at], RC.at[g, d - 1], s_rs.at[g, 2, d - 1], r_rs.at[g, 2, d - 1], peer(a1, d))
            )
    rel2.wait_recv()
    SHA[...] = jnp.zeros_like(SHA)
    for j in range(8):
        for k in range(2):
            SHA[:, pl.ds(640 * j + 256 * k, WIN)] += SHR[j, k].astype(F32)
    f_sent = []
    for g in range(3):
        for d in (1, 2, 3):
            rs[g, 2, d].wait_recv()
        tot = SB[g, pos[ORDERS[g][0]]].astype(F32) + SHA[:, cols(g, c)]
        for d in range(3):
            tot = tot + RC[g, d].astype(F32)
        FO[:, cols(g, c)] = tot.astype(BF)
        f_sent.append(go(remote(FO.at[:, cols(g, c)], FO.at[:, cols(g, c)], s_f.at[g], r_f.at[g], sibling)))
    for cp in f_sent:
        cp.wait_recv()
    res = FO[:, pl.ds(0, D)].astype(F32)
    out[...] = jnp.where(c == 0, res[:8], res[8:]).astype(BF)
    for cp in pend:
        cp.wait_send()


def local(tokens, gate_scores, expert_ids, expert_gate, expert_up, expert_down, shared_gate, shared_up, shared_down):
    ids = expert_ids.astype(BF)
    ext = jnp.concatenate(
        [ids, jnp.full((8, 2), -1, BF), gate_scores, jnp.zeros((8, EXT - 14), BF)], axis=1
    )
    vm, hbm = pl.BlockSpec(memory_space=pltpu.VMEM), pl.BlockSpec(memory_space=pl.ANY)
    dma = pltpu.SemaphoreType.DMA
    return pl.pallas_call(
        kernel,
        out_shape=jax.ShapeDtypeStruct((8, D), BF),
        in_specs=[vm, vm, hbm, hbm, hbm, vm, vm, vm],
        out_specs=vm,
        scratch_shapes=[
            pltpu.VMEM((4, 4, 4, 16, DX), BF),
            pltpu.VMEM((16, DX), BF),
            pltpu.VMEM((16, DX), BF),
            pltpu.VMEM((D, HALF), BF),
            pltpu.VMEM((D, HALF), BF),
            pltpu.VMEM((HALF, DX), BF),
            pltpu.VMEM((8, 96, WIN), BF),
            pltpu.VMEM((8, 2, 96, WIN), BF),
            pltpu.VMEM((96, D), BF),
            pltpu.VMEM((2, 8, 48, 512), BF),
            pltpu.VMEM((256, 1024), BF),
            pltpu.VMEM((1024, 256), BF),
            pltpu.VMEM((256, HALF), F32),
            pltpu.VMEM((256, HALF), F32),
            pltpu.VMEM((256, HALF), BF),
            pltpu.VMEM((3, 256, WID), BF),
            pltpu.VMEM((3, 256, WID), BF),
            pltpu.VMEM((3, 256, WID), BF),
            pltpu.VMEM((3, 4, 4, 4, 16, WID), BF),
            pltpu.VMEM((3, 3, 4, 4, 16, WID), BF),
            pltpu.VMEM((3, 4, 4, 16, WID), BF),
            pltpu.VMEM((3, 3, 4, 16, WID), BF),
            pltpu.VMEM((3, 4, 16, WID), BF),
            pltpu.VMEM((3, 3, 16, WID), BF),
            pltpu.VMEM((4, 256, WIN), BF),
            pltpu.VMEM((3, 256, WIN), BF),
            pltpu.VMEM((2, 128, WIN), BF),
            pltpu.VMEM((128, WIN), BF),
            pltpu.VMEM((8, 16, WIN), BF),
            pltpu.VMEM((8, 2, 16, WIN), BF),
            pltpu.VMEM((16, DX), F32),
            pltpu.VMEM((16, DX), BF),
            dma((3,)),
            dma((2,)),
            dma((3, 3, 3)), dma((3, 3, 3)),
            dma((3, 3, 3)), dma((3, 3, 3)),
            dma((7,)), dma((7,)),
            dma((7,)), dma((7,)),
            dma((4,)), dma((4,)),
            dma((7,)), dma((7,)),
            dma((3,)), dma((3,)),
            dma((3, 3, 3)), dma((3, 3, 3)),
            dma((3,)), dma((3,)),
            dma((3,)), dma((3,)),
        ],
        compiler_params=pltpu.CompilerParams(
            collective_id=0, has_side_effects=True, vmem_limit_bytes=62 * 2**20
        ),
        cost_estimate=pl.CostEstimate(flops=13 * 10**9, bytes_accessed=25 * 10**6, transcendentals=10**6),
    )(tokens, ext, expert_gate, expert_up, expert_down, shared_gate, shared_up, shared_down)


def solution(mesh):
    return jax.shard_map(
        local,
        mesh=mesh,
        in_specs=(
            P(("fsdp", "expert"), None),
            P(("fsdp", "expert"), None),
            P(("fsdp", "expert"), None),
            P(("fsdp", "expert"), None, None),
            P(("fsdp", "expert"), None, None),
            P(("fsdp", "expert"), None, None),
            P("expert", "fsdp"),
            P("expert", "fsdp"),
            P("fsdp", "expert"),
        ),
        out_specs=P(("fsdp", "expert"), None),
        check_vma=False,
    )
```

time: 273 us -> 123 us (0.45)
  Pallas kernels: 0 us -> 118 us
  blocking collectives: 114 us -> 0 us
  waiting for transfers between devices: 80.5 us -> 0 us
  matrix products: 29.6 us -> 0 us
  local copies, waits for them, and re-layouts: 20.8 us -> 3.51 us
  between operations: 13.3 us -> 0.01 us
  other arithmetic: 8.13 us -> 2.04 us
  starting transfers between devices: 4.96 us -> 0 us
    pallas_call x0 -> x1, Pallas kernels: none -> 118 us  [local(): pl.pallas_call(kernel, out_shape=jax.ShapeDtypeStruct((8, D), BF), in_spe...]
    reduce_scatter x1 -> x0, waiting for transfers between devices: 61.8 us -> none  [local(): lax.psum_scatter(shared_part, 'fsdp', scatter_dimension=0, tiled=True)]
    all_gather x1 -> x0, blocking collectives: 57.9 us -> none  [local(): col_tokens = lax.all_gather(tokens, 'fsdp', axis=0, tiled=True)]
    all_to_all x1 -> x0, blocking collectives: 56.5 us -> none  [local(): lax.all_to_all(outgoing, ('fsdp', 'expert'), split_axis=0, concat_axis=0,...]
    dot_general x4 -> x0, matrix products: 29.6 us -> none  [the longest x1 12.7 us: expert_rows(): jnp.dot(hidden, w_down, preferred_element_type=jnp.float32)]
    all_gather x3 -> x0, waiting for transfers between devices: 16.6 us -> none  [the longest x1 16.5 us: local(): lax.all_gather(shared_down, 'expert', axis=1, tiled=True)]
    reshape x3 -> x0, local copies, waits for them, and re-layouts: 9.55 us -> none  [the longest x1 6.29 us: expert_rows(): return result.reshape(block_shape)]
    gather x4 -> x0, local copies, waits for them, and re-layouts: 5.06 us -> none  [the longest x2 3.22 us: local(): jnp.take(half_sums, slot_place, axis=0)]
  transfers between devices with their start and end apart: 5 -> 0, of which waited for: 2 -> 0; matrix products, arithmetic and copies ran while one was open for 21% -> 0% of each run, Pallas kernels for 0% -> 0%
where the time goes in v1:
time: 123 us
  Pallas kernels  118 us (96%)
  local copies, waits for them, and re-layouts  3.51 us (3%)
  other arithmetic  2.04 us (2%)
    pallas_call x1, Pallas kernels, local(): pl.pallas_call(kernel, out_shape=jax.ShapeDtypeStruct((8, D), BF), in_spe...  118 us
    unnamed x2, local copies, waits for them, and re-layouts  3.35 us

profile of v1, /device:TPU:1, one launch (start us, length us, event | category | flops | bytes accessed | tf_op | source)
XLA Modules:
  0.0 123.1 jit_solution(10657164527458759737)
XLA Ops:
  0.0 0.1 pad.1.clone
  0.1 0.1 pad.3.clone
  0.2 0.7 convert_element_type.3
  0.9 1.4 %maximum_maximum_fusion.ext = bf16[8,256]{1,0:T(8,128)(2,1)} fusion(bf16[8,6]{1,0:T(8,128)(2,1)} %param.10, bf16[8,6]{1,0:T(8,128)(2,1)S(1)} %convert_element_type.3, bf16[256]{0:T(256)(128)(2,1)S(1)} %pad.3.clone, bf16[256]{0:T(256)(128)(2,1)S(1)} %pad.1.clone), kind=kLoop, calls=%fused_computation | loop fusion | flops 16384 | bytes 5312 | tf_op jit(solution)/shard_map/concatenate | solution.py:311
  2.2 1.8 %copy.10.sd = bf16[384,320]{1,0:T(8,128)(2,1)} copy(bf16[384,320]{0,1:T(8,128)(2,1)} %param.17) | data formatting | bytes 491520 | tf_op args[8]
  4.0 117.6 %shard_map.91 = bf16[8,5120]{1,0:T(8,128)(2,1)} custom-call(bf16[8,5120]{1,0:T(8,128)(2,1)} %tok.1, bf16[8,256]{1,0:T(8,128)(2,1)} %maximum_maximum_fusion.ext, bf16[1,5120,768]{2,1,0:T(8,128)(2,1)} %wg_h.1, bf16[1,5120,768]{2,1,0:T(8,128)(2,1)} %wu_h.1, bf16[1,768,5120]{2,1,0:T(8,128)(2,1)} %wd_h.1, bf16[320,384]{1,0:T(8,128)(2,1)} %sg.1, ...), custom_call_target="tpu_custom_call" | custom-call | flops 12999999488 | bytes 25000000 | tf_op jit(solution)/shard_map/pallas_call | solution.py:316
  121.6 1.5 %copy.12 = bf16[8,5120]{1,0:T(8,128)(2,1)} copy(bf16[8,5120]{1,0:T(8,128)(2,1)} %shard_map.91) | data formatting | bytes 163840
  (2 shorter events, 0.0 us)

commit v2 on v0

v2 whole, which is shorter than its diff:
```python
import jax
import jax.numpy as jnp
from jax import lax
from jax.experimental import pallas as pl
from jax.experimental.pallas import tpu as pltpu
from jax.sharding import PartitionSpec as P

MESH = pl.DeviceIdType.MESH
BF, F32 = jnp.bfloat16, jnp.float32
D, HALF_D, HALF, WIN = 5120, 2560, 768, 384
ORDERS = ((0, 1, 2), (1, 2, 0), (2, 0, 1))
OFF, WIDTH = (0, 896, 1792), (896, 896, 768)
DAY = (256, 64, 16)
NN, TN, NT = (((1,), (0,)), ((), ())), (((0,), (0,)), ((), ())), (((1,), (1,)), ((), ()))


def mm(a, b, dims=NN):
    return lax.dot_general(a, b, dims, preferred_element_type=F32)


def running(v, width):
    lane = lax.broadcasted_iota(jnp.int32, v.shape, 1)
    step = 1
    while step < width:
        v = v + jnp.where(lane >= step, pltpu.roll(v, step, 1), 0.0)
        step *= 2
    return v


def kernel(
    tok, gates, ids, wg_h, wu_h, wd_h, sg_h, su_h, sd_h, out,
    T, ID, stage, sib, e8, idst, idsib, wg, wu, wd, sg, su, sd, WS, WR, WA, SPS, SPR, SPO, HT,
    PM, GM, CT, XO, XR, ag, au, H, RO, PS, PR, XC, RA, SA, RB, SB, RC, SD, SDR, SZ, SZR, SQ, SHR, SHA, FO,
    lsem, s_sib, r_sib, s_id, r_id, s_a0, r_a0, s_a1, r_a1, s_a2, r_a2, s_w, r_w, s_sp, r_sp, s_x, r_x,
    s_h, r_h, s_rel, r_rel, s_p, r_p, s_sd, r_sd, s_q, r_q, s_rs, r_rs, s_f, r_f,
):
    f, e = lax.axis_index("fsdp"), lax.axis_index("expert")
    c = lax.rem(e, 2)
    y, x = f // 2, lax.rem(e // 2, 4)
    zh, zl = lax.rem(f, 2), e // 8
    pos = (y, zh * 2 + zl, x)
    chip = (y * 4 + pos[1]) * 4 + x
    mine = zl * 4 + x

    def dev(p, core):
        return (p[0] * 2 + p[1] // 2, (lax.rem(p[1], 2) * 4 + p[2]) * 2 + core)

    def peer(axis, dist):
        p = list(pos)
        p[axis] = lax.rem(p[axis] + dist, 4)
        return dev(p, c)

    def group(i):
        zz, xx = lax.rem(zl + i // 4, 2), lax.rem(x + i % 4, 4)
        return dev((y, zh * 2 + zz, xx), c), zz * 4 + xx

    def taker(i):
        zz, xx = lax.rem(zl + i // 4, 2), lax.rem(x + i % 4, 4)
        return dev((y, zh * 2 + zz, xx), zl), zz * 4 + xx

    def giver(i):
        return dev((y, zh * 2 + c, lax.rem(x + i % 4, 4)), lax.rem(c + i // 4, 2))

    sibling = dev(pos, 1 - c)

    def half(core, off, width):
        return pl.ds(pl.multiple_of(core * HALF_D + off, 128), width)

    def remote(src, dst, ss, rs, to):
        return pltpu.make_async_remote_copy(
            src_ref=src, dst_ref=dst, send_sem=ss, recv_sem=rs, device_id=to, device_id_type=MESH
        )

    pend = []

    def go(src, dst, ss, rs, to):
        cp = remote(src, dst, ss, rs, to)
        cp.start()
        pend.append(cp)
        return cp

    loads = [
        pltpu.make_async_copy(a, b, lsem.at[i])
        for i, (a, b) in enumerate(
            ((sg_h, sg), (su_h, su), (sd_h, sd), (wg_h.at[0], wg), (wu_h.at[0], wu), (wd_h.at[0], wd))
        )
    ]
    barrier = pltpu.get_barrier_semaphore()
    partners = [peer(a, d) for a in range(3) for d in (1, 2, 3)]
    partners += [group(i)[0] for i in (5, 6, 7)] + [sibling] + [giver(i) for i in range(1, 8)]
    for to in partners:
        pl.semaphore_signal(barrier, inc=1, device_id=to, device_id_type=MESH)

    @pl.when(zl != c)
    def _():
        pl.semaphore_signal(barrier, inc=1, device_id=giver(0), device_id_type=MESH)

    for ld in loads:
        ld.start()

    rows16 = lax.broadcasted_iota(jnp.int32, (16, 1), 0) // 8 == c
    v = tok[...].astype(F32)
    stage[...] = jnp.where(rows16, jnp.concatenate([v, v], 0), 0.0).astype(BF)
    e8[...] = jnp.full((8, 128), -1.0, F32)
    e8[:, pl.ds(0, 6)] = ids[...].astype(F32)
    e8[:, pl.ds(8, 6)] = gates[...].astype(F32)
    v = e8[...]
    idst[...] = jnp.where(rows16, jnp.concatenate([v, v], 0), 0.0).astype(BF)
    pl.semaphore_wait(barrier, len(partners) + jnp.where(zl != c, 1, 0))

    cp = go(idst, idsib, s_sib.at[0], r_sib.at[0], sibling)
    cp1 = go(stage.at[:, half(1 - c, 0, HALF_D)], sib, s_sib.at[1], r_sib.at[1], sibling)

    def view(ref, order, depth, col):
        ix = [slice(None)] * 3
        for a in order[depth:]:
            ix[a] = pos[a]
        return ref.at[ix[0], ix[1], ix[2], :, col]

    def id_send(s):
        v = view(ID, (0, 1, 2), s, slice(None))
        return [go(v, v, s_id.at[s, d - 1], r_id.at[s, d - 1], peer(s, d)) for d in (1, 2, 3)]

    cp.wait_recv()
    ID[pos[0], pos[1], pos[2]] = idst[...] + idsib[...]
    id_cp = id_send(0)
    cp1.wait_recv()
    T[pos[0], pos[1], pos[2]] = stage[:, half(c, 0, HALF_D)] + sib[...]

    a0, a1, a2 = {}, {}, {}
    for g in range(3):
        v = view(T, ORDERS[g], 0, pl.ds(OFF[g], WIDTH[g]))
        for d in (1, 3, 2):
            a0[g, d] = go(v, v, s_a0.at[g, d - 1], r_a0.at[g, d - 1], peer(ORDERS[g][0], d))

    def piece(g, k, back, part):
        b1, b2, b3 = ORDERS[g]
        cut = 128 * ((WIDTH[g] // 128 + 1 - k % 2) // 2)
        ix = [slice(None)] * 3
        ix[b2] = lax.rem(pos[b2] + 4 - k, 4)
        ix[b3] = lax.rem(pos[b3] + 4 - back, 4)
        col = pl.ds(OFF[g], cut) if part == 0 else pl.ds(OFF[g] + cut, WIDTH[g] - cut)
        return T.at[ix[0], ix[1], ix[2], :, col]

    def third(g, k, j):
        back, part, way = ((0, 0, 1), (0, 1, 3), (0, 1, 1), (0, 0, 3), (1, 0, 1), (3, 1, 3))[j]
        v = piece(g, k, back, part)
        a2[g, k, j] = go(v, v, s_a2.at[g, k, j], r_a2.at[g, k, j], peer(ORDERS[g][2], way))

    def slab(g, k):
        for j in range(4):
            third(g, k, j)

    def pass_on(k):
        for g in range(3):
            for j in (0, 1):
                a2[g, k, j].wait_recv()
                third(g, k, j + 4)

    for ld in loads[:3]:
        ld.wait()
    k_at = lax.broadcasted_iota(jnp.int32, (320, WIN), 0)
    l_at = lax.broadcasted_iota(jnp.int32, (320, WIN), 1)
    shift = (l_at == k_at + 64 * c).astype(F32).astype(BF)
    wt = mm(sg[...], shift, TN).astype(BF)
    for j in range(8):
        WS[j, pl.ds(0, 48)] = wt[48 * j : 48 * j + 48]
    wt = mm(su[...], shift, TN).astype(BF)
    for j in range(8):
        WS[j, pl.ds(48, 48)] = wt[48 * j : 48 * j + 48]

    def spread(src, dst, ss, rs):
        for i in range(1, 8):
            to, j = taker(i)
            go(src.at[j], dst.at[x, c], ss.at[i], rs.at[i % 4, c], to)

        @pl.when(zl != c)
        def _():
            to, j = taker(0)
            remote(src.at[j], dst.at[x, c], ss.at[0], rs.at[0, c], to).start()

        @pl.when(zl == c)
        def _():
            dst[x, c] = src[mine]

    def spread_recv(dst, rs):
        for i in range(1, 8):
            cc = lax.rem(c + i // 4, 2)
            pltpu.make_async_copy(dst.at[0, 0], dst.at[0, 0], rs.at[i % 4, cc]).wait()

        @pl.when(zl != c)
        def _():
            pltpu.make_async_copy(dst.at[0, 0], dst.at[0, 0], rs.at[0, c]).wait()

    def spread_end(src, ss):
        @pl.when(zl != c)
        def _():
            pltpu.make_async_copy(src.at[0], src.at[0], ss.at[0]).wait()

    spread(WS, WR, s_w, r_w)
    sdp = mm(sd[...], shift, TN).astype(BF)

    for cp in id_cp:
        cp.wait_recv()
    id_cp = id_send(1)
    for g in range(3):
        for d in (1, 3, 2):
            a0[g, d].wait_recv()
        v = view(T, ORDERS[g], 1, pl.ds(OFF[g], WIDTH[g]))
        for d in (1, 3, 2):
            a1[g, d] = go(v, v, s_a1.at[g, d - 1], r_a1.at[g, d - 1], peer(ORDERS[g][1], d))
    for g in range(3):
        slab(g, 0)
    for cp in id_cp:
        cp.wait_recv()
    id_cp = id_send(2)
    last = 0
    for k in (1, 3, 2):
        for g in range(3):
            a1[g, k].wait_recv()
            slab(g, k)
        pass_on(last)
        last = k
    pass_on(last)

    for cp in id_cp:
        cp.wait_recv()
    info = ID[...].reshape(1024, 128).astype(F32).T
    at = lax.broadcasted_iota(jnp.int32, (1, 1024), 1)
    hit = jnp.sum((info[0:8] == chip.astype(F32)).astype(F32), axis=0, keepdims=True)
    plane = [
        jnp.where(lax.rem(at // DAY[ORDERS[g][2]], 4) == p, hit, 0.0) for g in range(3) for p in range(4)
    ]
    run = running(jnp.concatenate(plane + [hit] * 4, 0), 1024) - 1.0
    slot = lax.broadcasted_iota(jnp.int32, (256, 1024), 0).astype(F32)
    PM[...] = jnp.where(slot == run[12:13], hit, 0.0).astype(BF)
    slot = lax.broadcasted_iota(jnp.int32, (64, 1024), 0).astype(F32)
    for g in range(3):
        pick = [jnp.where(slot == run[4 * g + p : 4 * g + p + 1], plane[4 * g + p], 0.0) for p in range(4)]
        GM[g] = mm(jnp.concatenate(pick, 0).astype(BF), PM[...], NT).astype(BF)
    slot = lax.broadcasted_iota(jnp.int32, (64, 256), 0).astype(F32)
    for g in range(3):
        b3 = ORDERS[g][2]
        ix = [slice(None)] * 3
        ix[b3] = pos[b3]
        info = ID[ix[0], ix[1], ix[2]].reshape(256, 128).astype(F32).T
        hits, weights = [], []
        for d in range(4):
            p = list(pos)
            p[b3] = lax.rem(p[b3] + 4 - d, 4)
            eq = (info[0:8] == ((p[0] * 4 + p[1]) * 4 + p[2]).astype(F32)).astype(F32)
            hits.append(jnp.sum(eq, axis=0, keepdims=True))
            weights.append(jnp.sum(eq * info[8:16], axis=0, keepdims=True))
        run = running(jnp.concatenate(hits + hits, 0), 256) - 1.0
        for d in range(4):
            CT[g, pl.ds(64 * d, 64)] = jnp.where(
                slot == run[d : d + 1], weights[d] * hits[d], 0.0
            ).astype(BF)

    spread_recv(WR, r_w)
    for j in range(4):
        o = 640 * j
        WA[:, pl.ds(o, 256)] = WR[j, 0, :, pl.ds(0, 256)]
        WA[:, pl.ds(o + 256, 128)] = WR[j, 0, :, pl.ds(256, 128)] + WR[j, 1, :, pl.ds(0, 128)]
        WA[:, pl.ds(o + 384, 256)] = WR[j, 1, :, pl.ds(128, 256)]
    for k in (0, 1, 3, 2):
        for g in range(3):
            for j in (2, 3, 4, 5):
                a2[g, k, j].wait_recv()

    def gate_up(core):
        def step(i, acc):
            col = pl.ds(pl.multiple_of(i * 640, 128), 640)
            return acc + mm(WA[:, col], T[pl.ds(2 * core, 2), :, :, :, col].reshape(512, 640), NT)

        return lax.fori_loop(0, 4, step, jnp.zeros((96, 512), F32))

    SPS[...] = gate_up(1 - c)
    sp = go(SPS, SPR, s_sp.at[0], r_sp.at[0], sibling)
    SPO[...] = gate_up(c)

    x_cp = []
    for i in range(4):
        col = pl.ds(640 * i, 640)
        XO[i] = mm(PM[...], T[:, :, :, :, col].reshape(1024, 640)).astype(BF)
        x_cp.append(go(XO.at[i], XR.at[i], s_x.at[i], r_x.at[i], sibling))

    sp.wait_recv()
    gu = SPO[...] + SPR[...]
    HT[c, mine] = (jax.nn.silu(gu[:48]) * gu[48:]).astype(BF)
    h_cp = []
    for i in range(1, 8):
        to, j = group(i)
        h_cp.append(go(HT.at[c, mine], HT.at[c, mine], s_h.at[i - 1], r_h.at[i - 1], to))

    loads[3].wait()
    loads[4].wait()
    ag[...] = jnp.zeros_like(ag)
    au[...] = jnp.zeros_like(au)

    def routed(ref, core, i):
        rows = pl.ds(pl.multiple_of(core * HALF_D + i * 640, 128), 640)
        ag[...] += mm(ref[i], wg[rows, :])
        au[...] += mm(ref[i], wu[rows, :])

    def own_part(i, _):
        routed(XO, c, i)
        return 0

    lax.fori_loop(0, 4, own_part, 0)
    for cp in x_cp:
        cp.wait_recv()

    def sib_part(i, _):
        routed(XR, 1 - c, i)
        return 0

    lax.fori_loop(0, 4, sib_part, 0)
    H[...] = (jax.nn.silu(ag[...]) * au[...]).astype(BF)

    for cp in h_cp:
        cp.wait_recv()
    rel = go(HT.at[c], HT.at[c], s_rel.at[0], r_rel.at[0], sibling)

    loads[5].wait()
    p_cp = []
    for g in range(3):
        w = pl.ds(0, WIDTH[g])
        PS[g, :, w] = mm(H[...], wd[:, half(1 - c, OFF[g], WIDTH[g])]).astype(BF)
        p_cp.append(go(PS.at[g, :, w], PR.at[g, :, w], s_p.at[g], r_p.at[g], sibling))

    rel.wait_recv()
    for t in range(2):
        part = mm(HT[t].reshape(384, 512), sdp, TN).astype(BF)
        for k in range(2):
            SD[2 * t + k] = part[256 * k : 256 * k + 256]
    sd_cp = []
    for d in (1, 2, 3):
        to = lax.rem(y + d, 4)
        sd_cp.append(go(SD.at[to], SDR.at[d - 1], s_sd.at[d - 1], r_sd.at[d - 1], peer(0, d)))

    for g in range(3):
        w = pl.ds(0, WIDTH[g])
        RO[g, :, w] = mm(H[...], wd[:, half(c, OFF[g], WIDTH[g])]).astype(BF)

    rs = {}
    for g in range(3):
        w = pl.ds(0, WIDTH[g])
        b3 = ORDERS[g][2]
        p_cp[g].wait_recv()
        both = (RO[g, :, w].astype(F32) + PR[g, :, w].astype(F32)).astype(BF)
        XC[g, :, :, w] = mm(GM[g], both).astype(BF).reshape(4, 64, WIDTH[g])
        for d in (1, 3, 2):
            to = lax.rem(pos[b3] + d, 4)
            rs[g, 0, d] = go(
                XC.at[g, to, :, w], RA.at[g, d, :, w], s_rs.at[g, 0, d - 1], r_rs.at[g, 0, d - 1], peer(b3, d)
            )
        RA[g, 0, :, w] = XC[g, pos[b3], :, w]

    for cp in sd_cp:
        cp.wait_recv()
    tot = SD[y].astype(F32)
    for d in range(3):
        tot = tot + SDR[d].astype(F32)
    tot = tot.astype(BF)
    SZ[0] = tot[:128]
    SZ[1] = tot[128:]
    z_cp = go(SZ.at[1 - zh], SZR, s_sd.at[3], r_sd.at[3], peer(1, 2))

    for g in range(3):
        w = pl.ds(0, WIDTH[g])
        _, b2, b3 = ORDERS[g]
        for d in (1, 3, 2):
            rs[g, 0, d].wait_recv()
        tot = mm(CT[g], RA[g, :, :, w].reshape(256, WIDTH[g]), TN)
        SA[g, :, :, :, w] = tot.astype(BF).reshape(4, 4, 16, WIDTH[g])
        first = min(a for a in range(3) if a != b3) == b2
        for d in (1, 3, 2):
            to = lax.rem(pos[b2] + d, 4)
            part = SA.at[g, to, :, :, w] if first else SA.at[g, :, to, :, w]
            rs[g, 1, d] = go(
                part, RB.at[g, d - 1, :, :, w], s_rs.at[g, 1, d - 1], r_rs.at[g, 1, d - 1], peer(b2, d)
            )

    z_cp.wait_recv()
    SQ[...] = (SZ[zh].astype(F32) + SZR[...].astype(F32)).astype(BF).reshape(8, 16, WIN)
    spread(SQ, SHR, s_q, r_q)

    for g in range(3):
        w = pl.ds(0, WIDTH[g])
        b1, b2, b3 = ORDERS[g]
        for d in (1, 3, 2):
            rs[g, 1, d].wait_recv()
        first = min(a for a in range(3) if a != b3) == b2
        tot = (SA[g, pos[b2], :, :, w] if first else SA[g, :, pos[b2], :, w]).astype(F32)
        for d in range(3):
            tot = tot + RB[g, d, :, :, w].astype(F32)
        SB[g, :, :, w] = tot.astype(BF)
        for d in (1, 3, 2):
            to = lax.rem(pos[b1] + d, 4)
            rs[g, 2, d] = go(
                SB.at[g, to, :, w], RC.at[g, d - 1, :, w], s_rs.at[g, 2, d - 1], r_rs.at[g, 2, d - 1], peer(b1, d)
            )

    spread_recv(SHR, r_q)
    SHA[...] = jnp.zeros_like(SHA)
    for j in range(4):
        for k in range(2):
            SHA[:, pl.ds(640 * j + 256 * k, WIN)] += SHR[j, k].astype(F32)
    f_cp = []
    for g in range(3):
        w = pl.ds(0, WIDTH[g])
        for d in (1, 3, 2):
            rs[g, 2, d].wait_recv()
        tot = SB[g, pos[ORDERS[g][0]], :, w].astype(F32) + SHA[:, pl.ds(OFF[g], WIDTH[g])]
        for d in range(3):
            tot = tot + RC[g, d, :, w].astype(F32)
        done = FO.at[:, half(c, OFF[g], WIDTH[g])]
        done[...] = tot.astype(BF)
        f_cp.append(go(done, done, s_f.at[g], r_f.at[g], sibling))
    for cp in f_cp:
        cp.wait_recv()
    res = FO[...].astype(F32)
    out[...] = jnp.where(c == 0, res[:8], res[8:]).astype(BF)
    for cp in pend:
        cp.wait_send()
    spread_end(WS, s_w)
    spread_end(SQ, s_q)


def local(tokens, gate_scores, expert_ids, expert_gate, expert_up, expert_down, shared_gate, shared_up, shared_down):
    vm, hbm = pl.BlockSpec(memory_space=pltpu.VMEM), pl.BlockSpec(memory_space=pl.ANY)

    def bf(*shape):
        return pltpu.VMEM(shape, BF)

    def f32(*shape):
        return pltpu.VMEM(shape, F32)

    def pair(*shape):
        return [pltpu.SemaphoreType.DMA(shape)] * 2

    return pl.pallas_call(
        kernel,
        out_shape=jax.ShapeDtypeStruct((8, D), BF),
        in_specs=[vm] * 3 + [hbm] * 6,
        out_specs=vm,
        scratch_shapes=[
            bf(4, 4, 4, 16, HALF_D), bf(4, 4, 4, 16, 128), bf(16, D), bf(16, HALF_D),
            f32(8, 128), bf(16, 128), bf(16, 128),
            bf(D, HALF), bf(D, HALF), bf(HALF, D), bf(320, 384), bf(320, 384), bf(320, 384),
            bf(8, 96, WIN), bf(4, 2, 96, WIN), bf(96, HALF_D),
            f32(96, 512), f32(96, 512), f32(96, 512), bf(2, 8, 48, 512),
            bf(256, 1024), bf(3, 256, 256), bf(3, 256, 256), bf(4, 256, 640), bf(4, 256, 640),
            f32(256, HALF), f32(256, HALF), bf(256, HALF),
            bf(3, 256, 896), bf(3, 256, 896), bf(3, 256, 896),
            bf(3, 4, 64, 896), bf(3, 4, 64, 896), bf(3, 4, 4, 16, 896), bf(3, 3, 4, 16, 896),
            bf(3, 4, 16, 896), bf(3, 3, 16, 896),
            bf(4, 256, WIN), bf(3, 256, WIN), bf(2, 128, WIN), bf(128, WIN), bf(8, 16, WIN),
            bf(4, 2, 16, WIN), f32(16, HALF_D), bf(16, D),
            pltpu.SemaphoreType.DMA((6,)),
            *pair(2), *pair(3, 3), *pair(3, 3), *pair(3, 3), *pair(3, 4, 6),
            pltpu.SemaphoreType.DMA((8,)), pltpu.SemaphoreType.DMA((4, 2)),
            *pair(1), *pair(4), *pair(7), *pair(1), *pair(3), *pair(4),
            pltpu.SemaphoreType.DMA((8,)), pltpu.SemaphoreType.DMA((4, 2)),
            *pair(3, 3, 3), *pair(3),
        ],
        compiler_params=pltpu.CompilerParams(
            collective_id=0, has_side_effects=True, vmem_limit_bytes=62 * 2**20
        ),
        cost_estimate=pl.CostEstimate(flops=13 * 10**9, bytes_accessed=25 * 10**6, transcendentals=10**6),
    )(
        tokens, gate_scores, expert_ids, expert_gate, expert_up, expert_down, shared_gate, shared_up, shared_down.T
    )


def solution(mesh):
    return jax.shard_map(
        local,
        mesh=mesh,
        in_specs=(
            P(("fsdp", "expert"), None),
            P(("fsdp", "expert"), None),
            P(("fsdp", "expert"), None),
            P(("fsdp", "expert"), None, None),
            P(("fsdp", "expert"), None, None),
            P(("fsdp", "expert"), None, None),
            P("expert", "fsdp"),
            P("expert", "fsdp"),
            P("fsdp", "expert"),
        ),
        out_specs=P(("fsdp", "expert"), None),
        check_vma=False,
    )
```

time: 273 us -> 92.6 us (0.34)
  blocking collectives: 114 us -> 0 us
  Pallas kernels: 0 us -> 90.8 us
  waiting for transfers between devices: 80.5 us -> 0 us
  matrix products: 29.6 us -> 0 us
  local copies, waits for them, and re-layouts: 20.8 us -> 1.53 us
  between operations: 13.3 us -> 0.01 us
  other arithmetic: 8.13 us -> 0 us
  starting transfers between devices: 4.96 us -> 0 us
    pallas_call x0 -> x1, Pallas kernels: none -> 90.8 us  [local(): pl.pallas_call(kernel, out_shape=jax.ShapeDtypeStruct((8, D), BF), in_spe...]
    reduce_scatter x1 -> x0, waiting for transfers between devices: 61.8 us -> none  [local(): lax.psum_scatter(shared_part, 'fsdp', scatter_dimension=0, tiled=True)]
    all_gather x1 -> x0, blocking collectives: 57.9 us -> none  [local(): col_tokens = lax.all_gather(tokens, 'fsdp', axis=0, tiled=True)]
    all_to_all x1 -> x0, blocking collectives: 56.5 us -> none  [local(): lax.all_to_all(outgoing, ('fsdp', 'expert'), split_axis=0, concat_axis=0,...]
    dot_general x4 -> x0, matrix products: 29.6 us -> none  [the longest x1 12.7 us: expert_rows(): jnp.dot(hidden, w_down, preferred_element_type=jnp.float32)]
    all_gather x3 -> x0, waiting for transfers between devices: 16.6 us -> none  [the longest x1 16.5 us: local(): lax.all_gather(shared_down, 'expert', axis=1, tiled=True)]
    reshape x3 -> x0, local copies, waits for them, and re-layouts: 9.55 us -> none  [the longest x1 6.29 us: expert_rows(): return result.reshape(block_shape)]
    gather x4 -> x0, local copies, waits for them, and re-layouts: 5.06 us -> none  [the longest x2 3.22 us: local(): jnp.take(half_sums, slot_place, axis=0)]
  transfers between devices with their start and end apart: 5 -> 0, of which waited for: 2 -> 0; matrix products, arithmetic and copies ran while one was open for 21% -> 0% of each run, Pallas kernels for 0% -> 0%
where the time goes in v2:
time: 92.6 us; the launch traced here: 92.4 us
  Pallas kernels  90.8 us (98%)
  local copies, waits for them, and re-layouts  1.53 us (2%)
    pallas_call x1, Pallas kernels, local(): pl.pallas_call(kernel, out_shape=jax.ShapeDtypeStruct((8, D), BF), in_spe...  90.8 us

profile of v2, /device:TPU:1, one launch (start us, length us, event | category | flops | bytes accessed | tf_op | source)
XLA Modules:
  0.0 92.4 jit_solution(2415132460681071496)
XLA Ops:
  0.0 90.8 %shard_map.91 = bf16[8,5120]{1,0:T(8,128)(2,1)} custom-call(bf16[8,5120]{1,0:T(8,128)(2,1)} %tok.1, bf16[8,6]{1,0:T(8,128)(2,1)} %gates.1, s32[8,6]{1,0:T(8,128)} %ids.1, bf16[1,5120,768]{2,1,0:T(8,128)(2,1)} %wg_h.1, bf16[1,5120,768]{2,1,0:T(8,128)(2,1)} %wu_h.1, bf16[1,768,5120]{2,1,0:T(8,128)(2,1)} %wd_h.1, bf16[320,384]{1,0:T(8,128)(2,1)} %sg_h.1, ...), custom_call_target="tpu_custom_call" | custom-call | flops 12999999488 | bytes 25000000 | tf_op jit(solution)/shard_map/pallas_call | solution.py:443
  90.9 1.5 %copy.11 = bf16[8,5120]{1,0:T(8,128)(2,1)} copy(bf16[8,5120]{1,0:T(8,128)(2,1)} %shard_map.91) | data formatting | bytes 163840

commit v3 on v2

v3 whole, which is shorter than its diff:
```python
import jax
import jax.numpy as jnp
from jax import lax
from jax.experimental import pallas as pl
from jax.experimental.pallas import tpu as pltpu
from jax.sharding import PartitionSpec as P

MESH = pl.DeviceIdType.MESH
BF, F32 = jnp.bfloat16, jnp.float32
D, HALF_D, HALF, WIN = 5120, 2560, 768, 384
ORDERS = ((0, 1, 2), (1, 2, 0), (2, 0, 1))
OFF, WIDTH = (0, 768, 1792), (768, 1024, 768)
ROFF, RWIDTH = (0, 1024, 1536), (1024, 512, 1024)
DAY = (256, 64, 16)
NN, TN, NT = (((1,), (0,)), ((), ())), (((0,), (0,)), ((), ())), (((1,), (1,)), ((), ()))


def mm(a, b, dims=NN):
    return lax.dot_general(a, b, dims, preferred_element_type=F32)


def running(v, width):
    lane = lax.broadcasted_iota(jnp.int32, v.shape, 1)
    step = 1
    while step < width:
        v = v + jnp.where(lane >= step, pltpu.roll(v, step, 1), 0.0)
        step *= 2
    return v


def kernel(
    tok, gates, ids, wg_h, wu_h, wd_h, sg_h, su_h, sd_h, out,
    T, ID, stage, sib, e8, idst, idsib, wg, wu, wd, sg, su, sd, WS, WR, WA, AC, SPR, HT,
    QF, QP, GM, CT, XP, XO, XR, ag, au, H, RO, PS, PR, XC, RA, SA, RB, SB, RC, SD, SDR, SZ, SZR, SQ, SHR, SHA, FO,
    lsem, s_sib, r_sib, s_id, r_id, s_a0, r_a0, s_a1, r_a1, s_a2, r_a2, s_w, r_w, s_sp, r_sp, s_x, r_x,
    s_h, r_h, s_rel, r_rel, s_p, r_p, s_sd, r_sd, s_q, r_q, s_rs, r_rs, s_f, r_f,
):
    f, e = lax.axis_index("fsdp"), lax.axis_index("expert")
    c = lax.rem(e, 2)
    y, x = f // 2, lax.rem(e // 2, 4)
    zh, zl = lax.rem(f, 2), e // 8
    pos = (y, zh * 2 + zl, x)
    chip = (y * 4 + pos[1]) * 4 + x
    mine = zl * 4 + x

    def dev(p, core):
        return (p[0] * 2 + p[1] // 2, (lax.rem(p[1], 2) * 4 + p[2]) * 2 + core)

    def peer(axis, dist):
        p = list(pos)
        p[axis] = lax.rem(p[axis] + dist, 4)
        return dev(p, c)

    def group(i):
        zz, xx = lax.rem(zl + i // 4, 2), lax.rem(x + i % 4, 4)
        return dev((y, zh * 2 + zz, xx), c), zz * 4 + xx

    def taker(i):
        zz, xx = lax.rem(zl + i // 4, 2), lax.rem(x + i % 4, 4)
        return dev((y, zh * 2 + zz, xx), zl), zz * 4 + xx

    def giver(i):
        return dev((y, zh * 2 + c, lax.rem(x + i % 4, 4)), lax.rem(c + i // 4, 2))

    sibling = dev(pos, 1 - c)

    def half(core, off, width):
        return pl.ds(pl.multiple_of(core * HALF_D + off, 128), width)

    def remote(src, dst, ss, rs, to):
        return pltpu.make_async_remote_copy(
            src_ref=src, dst_ref=dst, send_sem=ss, recv_sem=rs, device_id=to, device_id_type=MESH
        )

    pend = []

    def go(src, dst, ss, rs, to):
        cp = remote(src, dst, ss, rs, to)
        cp.start()
        pend.append(cp)
        return cp

    loads = [
        pltpu.make_async_copy(a, b, lsem.at[i])
        for i, (a, b) in enumerate(
            ((sg_h, sg), (su_h, su), (sd_h, sd), (wg_h.at[0], wg), (wu_h.at[0], wu), (wd_h.at[0], wd))
        )
    ]
    barrier = pltpu.get_barrier_semaphore()
    partners = [peer(a, d) for a in range(3) for d in (1, 2, 3)]
    partners += [group(i)[0] for i in (5, 6, 7)] + [sibling] + [giver(i) for i in range(1, 8)]
    for to in partners:
        pl.semaphore_signal(barrier, inc=1, device_id=to, device_id_type=MESH)

    @pl.when(zl != c)
    def _():
        pl.semaphore_signal(barrier, inc=1, device_id=giver(0), device_id_type=MESH)

    for ld in loads:
        ld.start()

    rows16 = lax.broadcasted_iota(jnp.int32, (16, 1), 0) // 8 == c
    v = tok[...].astype(F32)
    stage[...] = jnp.where(rows16, jnp.concatenate([v, v], 0), 0.0).astype(BF)
    e8[...] = jnp.full((8, 128), -1.0, F32)
    e8[:, pl.ds(0, 6)] = ids[...].astype(F32)
    e8[:, pl.ds(8, 6)] = gates[...].astype(F32)
    v = e8[...]
    idst[...] = jnp.where(rows16, jnp.concatenate([v, v], 0), 0.0).astype(BF)
    for ld in loads[:3]:
        ld.wait()
    k_at = lax.broadcasted_iota(jnp.int32, (320, WIN), 0)
    l_at = lax.broadcasted_iota(jnp.int32, (320, WIN), 1)
    shift = (l_at == k_at + 64 * c).astype(F32).astype(BF)
    wt = mm(sg[...], shift, TN).astype(BF)
    for j in range(8):
        WS[j, pl.ds(0, 48)] = wt[48 * j : 48 * j + 48]
    wt = mm(su[...], shift, TN).astype(BF)
    for j in range(8):
        WS[j, pl.ds(48, 48)] = wt[48 * j : 48 * j + 48]

    sdp = mm(sd[...], shift, TN).astype(BF)

    def spread(src, dst, ss, rs):
        for i in range(1, 8):
            to, j = taker(i)
            go(src.at[j], dst.at[x, c], ss.at[i], rs.at[i % 4, c], to)

        @pl.when(zl != c)
        def _():
            to, j = taker(0)
            remote(src.at[j], dst.at[x, c], ss.at[0], rs.at[0, c], to).start()

        @pl.when(zl == c)
        def _():
            dst[x, c] = src[mine]

    def spread_recv(dst, rs):
        for i in range(1, 8):
            cc = lax.rem(c + i // 4, 2)
            pltpu.make_async_copy(dst.at[0, 0], dst.at[0, 0], rs.at[i % 4, cc]).wait()

        @pl.when(zl != c)
        def _():
            pltpu.make_async_copy(dst.at[0, 0], dst.at[0, 0], rs.at[0, c]).wait()

    def spread_end(src, ss):
        @pl.when(zl != c)
        def _():
            pltpu.make_async_copy(src.at[0], src.at[0], ss.at[0]).wait()

    pl.semaphore_wait(barrier, len(partners) + jnp.where(zl != c, 1, 0))

    cp = go(idst, idsib, s_sib.at[0], r_sib.at[0], sibling)
    cp1 = go(stage.at[:, half(1 - c, 0, HALF_D)], sib, s_sib.at[1], r_sib.at[1], sibling)
    spread(WS, WR, s_w, r_w)

    def view(ref, order, depth, col):
        ix = [slice(None)] * 3
        for a in order[depth:]:
            ix[a] = pos[a]
        return ref.at[ix[0], ix[1], ix[2], :, col]

    def id_send(s):
        v = view(ID, (0, 1, 2), s, slice(None))
        return [go(v, v, s_id.at[s, d - 1], r_id.at[s, d - 1], peer(s, d)) for d in (1, 2, 3)]

    cp1.wait_recv()
    T[pos[0], pos[1], pos[2]] = stage[:, half(c, 0, HALF_D)] + sib[...]

    a0, a1, a2 = {}, {}, {}
    for g in range(3):
        v = view(T, ORDERS[g], 0, pl.ds(OFF[g], WIDTH[g]))
        for d in (1, 3, 2):
            a0[g, d] = go(v, v, s_a0.at[g, d - 1], r_a0.at[g, d - 1], peer(ORDERS[g][0], d))
    cp.wait_recv()
    ID[pos[0], pos[1], pos[2]] = idst[...] + idsib[...]
    id_cp = id_send(0)

    def piece(g, k, back, part):
        b1, b2, b3 = ORDERS[g]
        cut = 128 * ((WIDTH[g] // 128 + 1 - k % 2) // 2)
        ix = [slice(None)] * 3
        ix[b2] = lax.rem(pos[b2] + 4 - k, 4)
        ix[b3] = lax.rem(pos[b3] + 4 - back, 4)
        col = pl.ds(OFF[g], cut) if part == 0 else pl.ds(OFF[g] + cut, WIDTH[g] - cut)
        return T.at[ix[0], ix[1], ix[2], :, col]

    def third(g, k, j):
        back, part, way = ((0, 0, 1), (0, 1, 3), (0, 1, 1), (0, 0, 3), (1, 0, 1), (3, 1, 3))[j]
        v = piece(g, k, back, part)
        a2[g, k, j] = go(v, v, s_a2.at[g, k, j], r_a2.at[g, k, j], peer(ORDERS[g][2], way))

    def slab(g, k):
        for j in range(4):
            third(g, k, j)

    def pass_on(k):
        for g in range(3):
            for j in (0, 1):
                a2[g, k, j].wait_recv()
                third(g, k, j + 4)

    for g in range(3):
        for d in (1, 3, 2):
            a0[g, d].wait_recv()
        v = view(T, ORDERS[g], 1, pl.ds(OFF[g], WIDTH[g]))
        for d in (1, 3, 2):
            a1[g, d] = go(v, v, s_a1.at[g, d - 1], r_a1.at[g, d - 1], peer(ORDERS[g][1], d))
    for cp in id_cp:
        cp.wait_recv()
    id_cp = id_send(1)
    for g in range(3):
        slab(g, 0)

    for cp in id_cp:
        cp.wait_recv()
    id_cp = id_send(2)
    last = 0
    for k in (1, 3, 2):
        for g in range(3):
            a1[g, k].wait_recv()
            slab(g, k)
        pass_on(last)
        last = k
    pass_on(last)

    for cp in id_cp:
        cp.wait_recv()

    def ring_at(g, back):
        return lax.rem(pos[ORDERS[g][2]] + 4 - back, 4)

    def plane_ix(g, back):
        ix = [slice(None)] * 3
        ix[ORDERS[g][2]] = ring_at(g, back)
        return tuple(ix)

    def number(v):
        return v.astype(F32)

    def hits_of(info, expert):
        return (info[0:8] == number(expert)).astype(F32)

    def total(v):
        return jnp.sum(v, axis=0, keepdims=True)

    info = ID[...].reshape(1024, 128).astype(F32).T
    at = lax.broadcasted_iota(jnp.int32, (1, 1024), 1)
    hit = total(hits_of(info, chip))
    plane = [
        jnp.where(lax.rem(at // DAY[ORDERS[g][2]], 4) == ring_at(g, b), hit, 0.0) for g in range(3) for b in range(4)
    ]
    run = running(jnp.concatenate(plane + [hit] * 4, 0), 1024) - 1.0
    slot = lax.broadcasted_iota(jnp.int32, (64, 1024), 0).astype(F32)
    for g in range(3):
        for b in range(4):
            i = 4 * g + b
            QF[g, pl.ds(64 * b, 64)] = jnp.where(slot == run[i : i + 1], plane[i], 0.0).astype(BF)
    for g in (1, 2):
        GM[g - 1] = mm(QF[g], QF[0], NT).astype(BF)
    slot = lax.broadcasted_iota(jnp.int32, (64, 256), 0).astype(F32)
    for g in range(3):
        hits, weights, picks = [], [], []
        for b in range(4):
            info = ID[plane_ix(g, b)].reshape(256, 128).astype(F32).T
            picks.append(total(hits_of(info, chip)))
            if b == 0:
                for d in range(4):
                    p = list(pos)
                    p[ORDERS[g][2]] = ring_at(g, d)
                    eq = hits_of(info, (p[0] * 4 + p[1]) * 4 + p[2])
                    hits.append(total(eq))
                    weights.append(total(eq * info[8:16]))
        run = running(jnp.concatenate(hits + picks, 0), 256) - 1.0
        for d in range(4):
            CT[g, pl.ds(64 * d, 64)] = jnp.where(
                slot == run[d : d + 1], weights[d] * hits[d], 0.0
            ).astype(BF)
            QP[g, d] = jnp.where(slot == run[4 + d : 5 + d], picks[d], 0.0).astype(BF)

    spread_recv(WR, r_w)
    WA[...] = jnp.zeros_like(WA)
    for j in range(4):
        o = 640 * j
        for src, dst in ((0, 0), (48, 64)):
            r, w = pl.ds(src, 48), pl.ds(dst, 48)
            WA[w, pl.ds(o, 256)] = WR[j, 0, r, pl.ds(0, 256)]
            WA[w, pl.ds(o + 256, 128)] = WR[j, 0, r, pl.ds(256, 128)] + WR[j, 1, r, pl.ds(0, 128)]
            WA[w, pl.ds(o + 384, 256)] = WR[j, 1, r, pl.ds(128, 256)]

    AC[...] = jnp.zeros_like(AC)
    for b, js in ((0, ()), (1, (2,)), (3, (3,)), (2, (4, 5))):
        for g in range(3):
            for k in (0, 1, 3, 2):
                for j in js:
                    a2[g, k, j].wait_recv()
            ix, w, col = plane_ix(g, b), WIDTH[g], pl.ds(OFF[g], WIDTH[g])
            rows = T[(*ix, slice(None), col)].reshape(256, w)
            AC[ix] += mm(rows, WA[:, col], NT).reshape(4, 4, 16, 128)
            xp = mm(QP[g, b], rows).astype(BF)
            if g == 0:
                XO[pl.ds(64 * b, 64), col] = xp
            else:
                XP[g - 1, pl.ds(64 * b, 64), pl.ds(0, w)] = xp

    theirs = AC.at[pl.ds(2 * (1 - c), 2)]
    sp = go(theirs, SPR, s_sp.at[0], r_sp.at[0], sibling)

    x_cp = []
    for g in range(3):
        col = pl.ds(OFF[g], WIDTH[g])
        if g:
            XO[:, col] = mm(GM[g - 1], XP[g - 1, :, pl.ds(0, WIDTH[g])], TN).astype(BF)
        x_cp.append(go(XO.at[:, col], XR.at[:, col], s_x.at[g], r_x.at[g], sibling))

    loads[3].wait()
    loads[4].wait()
    ag[...] = jnp.zeros_like(ag)
    au[...] = jnp.zeros_like(au)

    def routed(ref, core, i):
        rows = pl.ds(pl.multiple_of(core * HALF_D + i * 512, 128), 512)
        part = ref[:, pl.ds(pl.multiple_of(i * 512, 128), 512)]
        ag[...] += mm(part, wg[rows, :])
        au[...] += mm(part, wu[rows, :])

    def own_part(i, _):
        routed(XO, c, i)
        return 0

    lax.fori_loop(0, 2, own_part, 0)
    sp.wait_recv()
    gu = (AC[pl.ds(2 * c, 2)] + SPR[...]).reshape(512, 128)
    hid = jax.nn.silu(gu) * pltpu.roll(gu, 64, 1)
    HT[c, mine] = hid.T[:48].astype(BF)
    h_cp = []
    for i in range(1, 8):
        to, j = group(i)
        h_cp.append(go(HT.at[c, mine], HT.at[c, mine], s_h.at[i - 1], r_h.at[i - 1], to))

    lax.fori_loop(2, 5, own_part, 0)
    for cp in x_cp:
        cp.wait_recv()

    def sib_part(i, _):
        routed(XR, 1 - c, i)
        return 0

    lax.fori_loop(0, 5, sib_part, 0)
    H[...] = (jax.nn.silu(ag[...]) * au[...]).astype(BF)
    for cp in h_cp:
        cp.wait_recv()
    rel = go(HT.at[c], HT.at[c], s_rel.at[0], r_rel.at[0], sibling)

    loads[5].wait()
    p_cp = []
    for g in range(3):
        w = pl.ds(0, RWIDTH[g])
        PS[g, :, w] = mm(H[...], wd[:, half(1 - c, ROFF[g], RWIDTH[g])]).astype(BF)
        p_cp.append(go(PS.at[g, :, w], PR.at[g, :, w], s_p.at[g], r_p.at[g], sibling))

    rel.wait_recv()
    for t in range(2):
        part = mm(HT[t].reshape(384, 512), sdp, TN).astype(BF)
        for k in range(2):
            SD[2 * t + k] = part[256 * k : 256 * k + 256]
    sd_cp = []
    for d in (1, 3, 2):
        to = lax.rem(y + d, 4)
        sd_cp.append(go(SD.at[to], SDR.at[d - 1], s_sd.at[d - 1], r_sd.at[d - 1], peer(0, d)))

    for g in range(3):
        w = pl.ds(0, RWIDTH[g])
        RO[g, :, w] = mm(H[...], wd[:, half(c, ROFF[g], RWIDTH[g])]).astype(BF)

    rs = {}
    for g in range(3):
        w = pl.ds(0, RWIDTH[g])
        b3 = ORDERS[g][2]
        p_cp[g].wait_recv()
        both = (RO[g, :, w].astype(F32) + PR[g, :, w].astype(F32)).astype(BF)
        if g:
            both = mm(GM[g - 1], both).astype(BF)
        XC[g, :, :, w] = both.reshape(4, 64, RWIDTH[g])
        for b in (3, 1, 2):
            rs[g, 0, b] = go(
                XC.at[g, b, :, w], RA.at[g, 4 - b, :, w], s_rs.at[g, 0, b - 1], r_rs.at[g, 0, b - 1], peer(b3, 4 - b)
            )
        RA[g, 0, :, w] = XC[g, 0, :, w]

    for cp in sd_cp:
        cp.wait_recv()
    tot = SD[y].astype(F32)
    for d in range(3):
        tot = tot + SDR[d].astype(F32)
    tot = tot.astype(BF)
    SZ[0] = tot[:128]
    SZ[1] = tot[128:]
    z_cp = go(SZ.at[1 - zh], SZR, s_sd.at[3], r_sd.at[3], peer(1, 2))

    z_cp.wait_recv()
    SQ[...] = (SZ[zh].astype(F32) + SZR[...].astype(F32)).astype(BF).reshape(8, 16, WIN)
    spread(SQ, SHR, s_q, r_q)

    for g in range(3):
        w = pl.ds(0, RWIDTH[g])
        _, b2, b3 = ORDERS[g]
        for d in (1, 3, 2):
            rs[g, 0, d].wait_recv()
        tot = mm(CT[g], RA[g, :, :, w].reshape(256, RWIDTH[g]), TN)
        SA[g, :, :, :, w] = tot.astype(BF).reshape(4, 4, 16, RWIDTH[g])
        first = min(a for a in range(3) if a != b3) == b2
        for d in (1, 3, 2):
            to = lax.rem(pos[b2] + d, 4)
            part = SA.at[g, to, :, :, w] if first else SA.at[g, :, to, :, w]
            rs[g, 1, d] = go(
                part, RB.at[g, d - 1, :, :, w], s_rs.at[g, 1, d - 1], r_rs.at[g, 1, d - 1], peer(b2, d)
            )

    for g in range(3):
        w = pl.ds(0, RWIDTH[g])
        b1, b2, b3 = ORDERS[g]
        for d in (1, 3, 2):
            rs[g, 1, d].wait_recv()
        first = min(a for a in range(3) if a != b3) == b2
        tot = (SA[g, pos[b2], :, :, w] if first else SA[g, :, pos[b2], :, w]).astype(F32)
        for d in range(3):
            tot = tot + RB[g, d, :, :, w].astype(F32)
        SB[g, :, :, w] = tot.astype(BF)
        for d in (1, 3, 2):
            to = lax.rem(pos[b1] + d, 4)
            rs[g, 2, d] = go(
                SB.at[g, to, :, w], RC.at[g, d - 1, :, w], s_rs.at[g, 2, d - 1], r_rs.at[g, 2, d - 1], peer(b1, d)
            )

    spread_recv(SHR, r_q)
    SHA[...] = jnp.zeros_like(SHA)
    for j in range(4):
        for k in range(2):
            SHA[:, pl.ds(640 * j + 256 * k, WIN)] += SHR[j, k].astype(F32)
    f_cp = []
    for g in range(3):
        w = pl.ds(0, RWIDTH[g])
        for d in (1, 3, 2):
            rs[g, 2, d].wait_recv()
        tot = SB[g, pos[ORDERS[g][0]], :, w].astype(F32) + SHA[:, pl.ds(ROFF[g], RWIDTH[g])]
        for d in range(3):
            tot = tot + RC[g, d, :, w].astype(F32)
        done = FO.at[:, half(c, ROFF[g], RWIDTH[g])]
        done[...] = tot.astype(BF)
        f_cp.append(go(done, done, s_f.at[g], r_f.at[g], sibling))
    for cp in f_cp:
        cp.wait_recv()
    res = FO[...].astype(F32)
    out[...] = jnp.where(c == 0, res[:8], res[8:]).astype(BF)
    for cp in pend:
        cp.wait_send()
    spread_end(WS, s_w)
    spread_end(SQ, s_q)


def local(tokens, gate_scores, expert_ids, expert_gate, expert_up, expert_down, shared_gate, shared_up, shared_down):
    vm, hbm = pl.BlockSpec(memory_space=pltpu.VMEM), pl.BlockSpec(memory_space=pl.ANY)

    def bf(*shape):
        return pltpu.VMEM(shape, BF)

    def f32(*shape):
        return pltpu.VMEM(shape, F32)

    def pair(*shape):
        return [pltpu.SemaphoreType.DMA(shape)] * 2

    return pl.pallas_call(
        kernel,
        out_shape=jax.ShapeDtypeStruct((8, D), BF),
        in_specs=[vm] * 3 + [hbm] * 6,
        out_specs=vm,
        scratch_shapes=[
            bf(4, 4, 4, 16, HALF_D), bf(4, 4, 4, 16, 128), bf(16, D), bf(16, HALF_D),
            f32(8, 128), bf(16, 128), bf(16, 128),
            bf(D, HALF), bf(D, HALF), bf(HALF, D), bf(320, 384), bf(320, 384), bf(320, 384),
            bf(8, 96, WIN), bf(4, 2, 96, WIN), bf(128, HALF_D),
            f32(4, 4, 4, 16, 128), f32(2, 4, 4, 16, 128), bf(2, 8, 48, 512),
            bf(3, 256, 1024), bf(3, 4, 64, 256), bf(2, 256, 256), bf(3, 256, 256),
            bf(2, 256, 1024), bf(256, HALF_D), bf(256, HALF_D),
            f32(256, HALF), f32(256, HALF), bf(256, HALF),
            bf(3, 256, 1024), bf(3, 256, 1024), bf(3, 256, 1024),
            bf(3, 4, 64, 1024), bf(3, 4, 64, 1024), bf(3, 4, 4, 16, 1024), bf(3, 3, 4, 16, 1024),
            bf(3, 4, 16, 1024), bf(3, 3, 16, 1024),
            bf(4, 256, WIN), bf(3, 256, WIN), bf(2, 128, WIN), bf(128, WIN), bf(8, 16, WIN),
            bf(4, 2, 16, WIN), f32(16, HALF_D), bf(16, D),
            pltpu.SemaphoreType.DMA((6,)),
            *pair(2), *pair(3, 3), *pair(3, 3), *pair(3, 3), *pair(3, 4, 6),
            pltpu.SemaphoreType.DMA((8,)), pltpu.SemaphoreType.DMA((4, 2)),
            *pair(1), *pair(3), *pair(7), *pair(1), *pair(3), *pair(4),
            pltpu.SemaphoreType.DMA((8,)), pltpu.SemaphoreType.DMA((4, 2)),
            *pair(3, 3, 3), *pair(3),
        ],
        compiler_params=pltpu.CompilerParams(
            collective_id=0, has_side_effects=True, vmem_limit_bytes=62 * 2**20
        ),
        cost_estimate=pl.CostEstimate(flops=13 * 10**9, bytes_accessed=25 * 10**6, transcendentals=10**6),
    )(
        tokens, gate_scores, expert_ids, expert_gate, expert_up, expert_down, shared_gate, shared_up, shared_down.T
    )


def solution(mesh):
    return jax.shard_map(
        local,
        mesh=mesh,
        in_specs=(
            P(("fsdp", "expert"), None),
            P(("fsdp", "expert"), None),
            P(("fsdp", "expert"), None),
            P(("fsdp", "expert"), None, None),
            P(("fsdp", "expert"), None, None),
            P(("fsdp", "expert"), None, None),
            P("expert", "fsdp"),
            P("expert", "fsdp"),
            P("fsdp", "expert"),
        ),
        out_specs=P(("fsdp", "expert"), None),
        check_vma=False,
    )
```

time: 92.6 us -> 91.6 us (0.989)
    pallas_call x1, Pallas kernels: 90.8 us -> 89.9 us  [local(): pl.pallas_call(kernel, out_shape=jax.ShapeDtypeStruct((8, D), BF), in_spe...]
where the time goes in v3:
time: 91.6 us; the launch traced here: 91.5 us
  Pallas kernels  89.9 us (98%)
  local copies, waits for them, and re-layouts  1.53 us (2%)
    pallas_call x1, Pallas kernels, local(): pl.pallas_call(kernel, out_shape=jax.ShapeDtypeStruct((8, D), BF), in_spe...  89.9 us

profile of v3, /device:TPU:1, one launch (start us, length us, event | category | flops | bytes accessed | tf_op | source)
XLA Modules:
  0.0 91.5 jit_solution(8287645497132543103)
XLA Ops:
  0.0 89.9 %shard_map.91 = bf16[8,5120]{1,0:T(8,128)(2,1)} custom-call(bf16[8,5120]{1,0:T(8,128)(2,1)} %tok.1, bf16[8,6]{1,0:T(8,128)(2,1)} %gates.1, s32[8,6]{1,0:T(8,128)} %ids.1, bf16[1,5120,768]{2,1,0:T(8,128)(2,1)} %wg_h.1, bf16[1,5120,768]{2,1,0:T(8,128)(2,1)} %wu_h.1, bf16[1,768,5120]{2,1,0:T(8,128)(2,1)} %wd_h.1, bf16[320,384]{1,0:T(8,128)(2,1)} %sg_h.1, ...), custom_call_target="tpu_custom_call" | custom-call | flops 12999999488 | bytes 25000000 | tf_op jit(solution)/shard_map/pallas_call | solution.py:475
  89.9 1.5 %copy.11 = bf16[8,5120]{1,0:T(8,128)(2,1)} copy(bf16[8,5120]{1,0:T(8,128)(2,1)} %shard_map.91) | data formatting | bytes 163840

commit v4 on v3

--- a/solution.py
+++ b/solution.py
@@ -31,7 +31,7 @@
 def kernel(
     tok, gates, ids, wg_h, wu_h, wd_h, sg_h, su_h, sd_h, out,
     T, ID, stage, sib, e8, idst, idsib, wg, wu, wd, sg, su, sd, WS, WR, WA, AC, SPR, HT,
-    QF, QP, GM, CT, XP, XO, XR, ag, au, H, RO, PS, PR, XC, RA, SA, RB, SB, RC, SD, SDR, SZ, SZR, SQ, SHR, SHA, FO,
+    QF, QP, GM, CT, XP, XO, XR, ag, au, H, RO, PS, PR, XC, RA, SA, RB, SB, RC, SD, SDR, SZ, SZR, ZB, ZS, ZR, SQ, SHR, SHA, FO,
     lsem, s_sib, r_sib, s_id, r_id, s_a0, r_a0, s_a1, r_a1, s_a2, r_a2, s_w, r_w, s_sp, r_sp, s_x, r_x,
     s_h, r_h, s_rel, r_rel, s_p, r_p, s_sd, r_sd, s_q, r_q, s_rs, r_rs, s_f, r_f,
 ):
@@ -353,6 +353,11 @@
         cp.wait_recv()
     rel = go(HT.at[c], HT.at[c], s_rel.at[0], r_rel.at[0], sibling)
 
+    LOW, TOP = pl.ds(0, 256), pl.ds(256, 128)
+
+    def z_rows(at):
+        return pl.ds(pl.multiple_of(at * 128, 128), 128)
+
     loads[5].wait()
     p_cp = []
     for g in range(3):
@@ -365,10 +370,13 @@
         part = mm(HT[t].reshape(384, 512), sdp, TN).astype(BF)
         for k in range(2):
             SD[2 * t + k] = part[256 * k : 256 * k + 256]
+    zb = go(SD.at[:, z_rows(1 - zh), TOP], ZB, s_sd.at[4], r_sd.at[4], peer(1, 2))
     sd_cp = []
     for d in (1, 3, 2):
         to = lax.rem(y + d, 4)
-        sd_cp.append(go(SD.at[to], SDR.at[d - 1], s_sd.at[d - 1], r_sd.at[d - 1], peer(0, d)))
+        sd_cp.append(
+            go(SD.at[to, :, LOW], SDR.at[d - 1, :, LOW], s_sd.at[d - 1], r_sd.at[d - 1], peer(0, d))
+        )
 
     for g in range(3):
         w = pl.ds(0, RWIDTH[g])
@@ -389,18 +397,31 @@
             )
         RA[g, 0, :, w] = XC[g, 0, :, w]
 
+    zb.wait_recv()
+    ZS[...] = (SD[:, z_rows(zh), TOP].astype(F32) + ZB[...].astype(F32)).astype(BF)
+    zy = []
+    for d in (1, 3, 2):
+        to = lax.rem(y + d, 4)
+        zy.append(go(ZS.at[to], ZR.at[d - 1], s_sd.at[4 + d], r_sd.at[4 + d], peer(0, d)))
+
     for cp in sd_cp:
         cp.wait_recv()
-    tot = SD[y].astype(F32)
+    tot = SD[y, :, LOW].astype(F32)
     for d in range(3):
-        tot = tot + SDR[d].astype(F32)
+        tot = tot + SDR[d, :, LOW].astype(F32)
     tot = tot.astype(BF)
     SZ[0] = tot[:128]
     SZ[1] = tot[128:]
     z_cp = go(SZ.at[1 - zh], SZR, s_sd.at[3], r_sd.at[3], peer(1, 2))
 
     z_cp.wait_recv()
-    SQ[...] = (SZ[zh].astype(F32) + SZR[...].astype(F32)).astype(BF).reshape(8, 16, WIN)
+    SQ[:, :, LOW] = (SZ[zh].astype(F32) + SZR[...].astype(F32)).astype(BF).reshape(8, 16, 256)
+    for cp in zy:
+        cp.wait_recv()
+    tot = ZS[y].astype(F32)
+    for d in range(3):
+        tot = tot + ZR[d].astype(F32)
+    SQ[:, :, TOP] = tot.astype(BF).reshape(8, 16, 128)
     spread(SQ, SHR, s_q, r_q)
 
     for g in range(3):
@@ -489,12 +510,12 @@
             bf(3, 256, 1024), bf(3, 256, 1024), bf(3, 256, 1024),
             bf(3, 4, 64, 1024), bf(3, 4, 64, 1024), bf(3, 4, 4, 16, 1024), bf(3, 3, 4, 16, 1024),
             bf(3, 4, 16, 1024), bf(3, 3, 16, 1024),
-            bf(4, 256, WIN), bf(3, 256, WIN), bf(2, 128, WIN), bf(128, WIN), bf(8, 16, WIN),
+            bf(4, 256, WIN), bf(3, 256, WIN), bf(2, 128, 256), bf(128, 256), bf(4, 128, 128), bf(4, 128, 128), bf(3, 128, 128), bf(8, 16, WIN),
             bf(4, 2, 16, WIN), f32(16, HALF_D), bf(16, D),
             pltpu.SemaphoreType.DMA((6,)),
             *pair(2), *pair(3, 3), *pair(3, 3), *pair(3, 3), *pair(3, 4, 6),
             pltpu.SemaphoreType.DMA((8,)), pltpu.SemaphoreType.DMA((4, 2)),
-            *pair(1), *pair(3), *pair(7), *pair(1), *pair(3), *pair(4),
+            *pair(1), *pair(3), *pair(7), *pair(1), *pair(3), *pair(8),
             pltpu.SemaphoreType.DMA((8,)), pltpu.SemaphoreType.DMA((4, 2)),
             *pair(3, 3, 3), *pair(3),
         ],

time: 91.6 us -> 89.4 us (0.976)
  Pallas kernels: 89.9 us -> 87.7 us
    pallas_call x1, Pallas kernels: 89.9 us -> 87.7 us  [local(): pl.pallas_call(kernel, out_shape=jax.ShapeDtypeStruct((8, D), BF), in_spe...]
where the time goes in v4:
time: 89.4 us; the launch traced here: 89.2 us
  Pallas kernels  87.7 us (98%)
  local copies, waits for them, and re-layouts  1.53 us (2%)
    pallas_call x1, Pallas kernels, local(): pl.pallas_call(kernel, out_shape=jax.ShapeDtypeStruct((8, D), BF), in_spe...  87.7 us

profile of v4, /device:TPU:1, one launch (start us, length us, event | category | flops | bytes accessed | tf_op | source)
XLA Modules:
  0.0 89.2 jit_solution(13844986641503038580)
XLA Ops:
  0.0 87.7 %shard_map.91 = bf16[8,5120]{1,0:T(8,128)(2,1)} custom-call(bf16[8,5120]{1,0:T(8,128)(2,1)} %tok.1, bf16[8,6]{1,0:T(8,128)(2,1)} %gates.1, s32[8,6]{1,0:T(8,128)} %ids.1, bf16[1,5120,768]{2,1,0:T(8,128)(2,1)} %wg_h.1, bf16[1,5120,768]{2,1,0:T(8,128)(2,1)} %wu_h.1, bf16[1,768,5120]{2,1,0:T(8,128)(2,1)} %wd_h.1, bf16[320,384]{1,0:T(8,128)(2,1)} %sg_h.1, ...), custom_call_target="tpu_custom_call" | custom-call | flops 12999999488 | bytes 25000000 | tf_op jit(solution)/shard_map/pallas_call | solution.py:496
  87.7 1.5 %copy.11 = bf16[8,5120]{1,0:T(8,128)(2,1)} copy(bf16[8,5120]{1,0:T(8,128)(2,1)} %shard_map.91) | data formatting | bytes 163840
